TPU v7x, 128 devices: a whole 4x4x4 slice. The times are simulated.
128 devices in a mesh: ctx: 16 (over z, x), tp: 8 (over y, core).
Axes of the slice: x: 4, y: 4, z: 4, core: 2. Of those that a mesh axis runs over, the one named last changes fastest.
Arguments:
- q_raw: bfloat16 [4096, 5120], P('ctx', 'tp'), may hold values from -300 to 300
- k_raw: bfloat16 [4096, 1024], P('ctx', 'tp'), may hold values from -300 to 300
- values: bfloat16 [4096, 1024], P('ctx', 'tp'), may hold values from -6 to 6
- d_out: bfloat16 [4096, 5120], P('ctx', 'tp'), may hold values from -24 to 24
- q_gain: float32 [5120], P('tp'), may hold values from 0.7 to 2
- k_gain: float32 [1024], P('tp'), may hold values from 0.7 to 2
- span_order: int32 [32], replicated, may hold values from 0 to 31, as said below
Outputs:
- d_q_raw: bfloat16 [4096, 5120], P('ctx', 'tp')
- d_k_raw: bfloat16 [4096, 1024], P('ctx', 'tp')
- d_values: bfloat16 [4096, 1024], P('ctx', 'tp')
- d_q_gain: float32 [5120], P('tp')
- d_k_gain: float32 [1024], P('tp')
Inputs may be any that keep to these rules, and one draw needn't show every extreme that they name: `span_order`: each span number appears once; slots 2c and 2c + 1 hold two spans that sum to 31.
All inputs are finite; a program needn't handle non-finite values.
Results may differ from a plain program's by a relative error of at most 0.012.
The roundings to bfloat16 on the way count: a program that leaves them out, or rounds other values in their place, can miss the bound.
Values may be sent and summed in bfloat16 or wider, within the bound.
A program may use at most 64 MiB of HBM per device.

v0:
```python
import jax
import jax.numpy as jnp
from jax import lax
from jax.sharding import PartitionSpec as P

D = 5120
DH = 128
KEY_BLOCK = 1024
SPAN = 128
KVD = 1024


EPS = 1e-06
THETA = 500000.0
NEG = -1e30


def lookup(entries, slots_in):
    matches = slots_in[:, None] == jnp.arange(entries.shape[0], dtype=jnp.int32)[None, :]
    return jnp.sum(jnp.where(matches, entries[None, :], 0), axis=1)


def token_positions(span_order, start_row, total_rows):
    row_ids = start_row + jnp.arange(total_rows, dtype=jnp.int32)
    return lookup(span_order, row_ids // SPAN) * SPAN + row_ids % SPAN


def rotate(tensor, positions, direction_sign):
    half_width = tensor.shape[-1] // 2
    frequency = THETA ** (-jnp.arange(half_width, dtype=jnp.float32) / half_width)
    angles = positions.astype(jnp.float32)[:, None] * frequency[None, :]
    cos_part = jnp.cos(angles)[:, None, :]
    sin_part = direction_sign * jnp.sin(angles)[:, None, :]
    leading = tensor[..., :half_width]
    trailing = tensor[..., half_width:]
    return jnp.concatenate(
        [leading * cos_part - trailing * sin_part, trailing * cos_part + leading * sin_part],
        axis=-1,
    )


def tile_scores(queries, key_rows, query_pos, key_pos):
    scores = jnp.einsum(
        "rkgd,nkd->kgrn", queries, key_rows, preferred_element_type=jnp.float32
    ) * DH ** (-0.5)
    return (scores, key_pos[None, :] <= query_pos[:, None])


def forward_tile(carried, queries, grads_out, key_rows, value_rows, query_pos, key_pos):
    run_max, run_sum, run_dot = carried
    scores, allowed = tile_scores(queries, key_rows, query_pos, key_pos)
    masked = jnp.where(allowed, scores, NEG)
    new_max = jnp.maximum(run_max, jnp.max(masked, axis=-1))
    weights = jnp.where(allowed, jnp.exp(masked - new_max[..., None]), 0.0)
    d_probs = jnp.einsum(
        "rkgd,nkd->kgrn", grads_out, value_rows, preferred_element_type=jnp.float32
    )
    factor = jnp.exp(run_max - new_max)
    return (
        new_max,
        run_sum * factor + jnp.sum(weights, axis=-1),
        run_dot * factor + jnp.sum(weights * d_probs, axis=-1),
    )


def backward_tile(
    queries, grads_out, log_total, row_delta, key_rows, value_rows, query_pos, key_pos
):
    scores, allowed = tile_scores(queries, key_rows, query_pos, key_pos)
    probs = jnp.where(allowed, jnp.exp(scores - log_total[..., None]), 0.0)
    d_probs = jnp.einsum(
        "rkgd,nkd->kgrn", grads_out, value_rows, preferred_element_type=jnp.float32
    )
    d_scores = probs * (d_probs - row_delta[..., None])
    return (probs.astype(jnp.bfloat16), d_scores.astype(jnp.bfloat16))


def when_visible(compute, carried, query_pos, key_pos):

    def unchanged(current):
        return current

    return lax.cond(jnp.min(key_pos) > jnp.max(query_pos), unchanged, compute, carried)


def in_blocks(update, carried, arrays, start_row):
    total_rows = arrays[0].shape[0]
    block_rows = KEY_BLOCK

    def advance(number, current):
        offset = number * block_rows
        pieces = tuple(
            (
                lax.dynamic_slice_in_dim(member_array, offset, block_rows, 0)
                for member_array in arrays
            )
        )
        return update(current, pieces, start_row + offset, offset)

    return lax.fori_loop(0, total_rows // block_rows, advance, carried)


def per_device(q_raw, k_raw, values, d_out, q_gain, k_gain, span_order):
    local_rows = q_raw.shape[0]
    kv_heads = k_raw.shape[1] // DH
    q_heads = q_raw.shape[1] // DH
    group_size = q_heads // kv_heads
    all_rows = local_rows * lax.axis_size("ctx")
    own_pos = token_positions(span_order, lax.axis_index("ctx") * local_rows, local_rows)
    q_float = q_raw.astype(jnp.float32)
    k_float = k_raw.astype(jnp.float32)
    q_squares, k_squares = lax.psum(
        (jnp.sum(q_float * q_float, axis=1), jnp.sum(k_float * k_float, axis=1)), "tp"
    )
    q_inv = lax.rsqrt(q_squares / D + EPS)
    k_inv = lax.rsqrt(k_squares / KVD + EPS)
    q_hat = q_float * q_inv[:, None]
    k_hat = k_float * k_inv[:, None]
    q_rot = (
        rotate((q_hat * q_gain[None, :]).reshape(local_rows, q_heads, DH), own_pos, 1.0)
        .astype(jnp.bfloat16)
        .reshape(local_rows, kv_heads, group_size, DH)
    )
    k_rot = rotate(
        (k_hat * k_gain[None, :]).reshape(local_rows, kv_heads, DH), own_pos, 1.0
    ).astype(jnp.bfloat16)
    v_heads = values.reshape(local_rows, kv_heads, DH)
    o_heads = d_out.reshape(local_rows, kv_heads, group_size, DH)
    stat_shape = (kv_heads, group_size, local_rows)
    stat_init = (
        jnp.full(stat_shape, NEG, jnp.float32),
        jnp.zeros(stat_shape, jnp.float32),
        jnp.zeros(stat_shape, jnp.float32),
    )

    def forward_update(carried, pieces, start_row, offset):
        key_pos = token_positions(span_order, start_row, pieces[0].shape[0])

        def compute(current):
            return forward_tile(current, q_rot, o_heads, pieces[0], pieces[1], own_pos, key_pos)

        return when_visible(compute, carried, own_pos, key_pos)

    all_keys, all_values = (
        lax.all_gather(k_rot, "ctx", axis=0, tiled=True),
        lax.all_gather(v_heads, "ctx", axis=0, tiled=True),
    )
    run_max, run_sum, run_dot = in_blocks(forward_update, stat_init, (all_keys, all_values), 0)
    log_total = run_max + jnp.log(run_sum)
    row_delta = run_dot / run_sum

    def backward_update(carried, pieces, start_row, offset):
        key_pos = token_positions(span_order, start_row, pieces[0].shape[0])

        def compute(current):
            probs_b, d_scores_b = backward_tile(
                q_rot, o_heads, log_total, row_delta, pieces[0], pieces[1], own_pos, key_pos
            )
            d_query = current[0] + jnp.einsum(
                "kgrn,nkd->rkgd", d_scores_b, pieces[0], preferred_element_type=jnp.float32
            ) * DH ** (-0.5)
            d_key = jnp.einsum(
                "kgrn,rkgd->nkd", d_scores_b, q_rot, preferred_element_type=jnp.float32
            ) * DH ** (-0.5)
            d_value = jnp.einsum(
                "kgrn,rkgd->nkd", probs_b, o_heads, preferred_element_type=jnp.float32
            )
            return (
                d_query,
                lax.dynamic_update_slice_in_dim(current[1], d_key, start_row, 0),
                lax.dynamic_update_slice_in_dim(current[2], d_value, start_row, 0),
            )

        return when_visible(compute, carried, own_pos, key_pos)

    d_query_init = jnp.zeros((local_rows, kv_heads, group_size, DH), jnp.float32)
    grad_init = (
        d_query_init,
        jnp.zeros((all_rows, kv_heads, DH), jnp.float32),
        jnp.zeros((all_rows, kv_heads, DH), jnp.float32),
    )
    gradients = in_blocks(backward_update, grad_init, (all_keys, all_values), 0)
    own_dk, own_dv = (
        lax.psum_scatter(gradients[1], "ctx", scatter_dimension=0, tiled=True),
        lax.psum_scatter(gradients[2], "ctx", scatter_dimension=0, tiled=True),
    )
    d_q_norm = rotate(gradients[0].reshape(local_rows, q_heads, DH), own_pos, -1.0).reshape(
        local_rows, q_heads * DH
    )
    d_k_norm = rotate(own_dk, own_pos, -1.0).reshape(local_rows, kv_heads * DH)
    q_scaled = d_q_norm * q_gain[None, :]
    k_scaled = d_k_norm * k_gain[None, :]
    q_inner, k_inner = lax.psum(
        (jnp.sum(q_scaled * q_hat, axis=1), jnp.sum(k_scaled * k_hat, axis=1)), "tp"
    )
    d_q_gain, d_k_gain = lax.psum(
        (jnp.sum(d_q_norm * q_hat, axis=0), jnp.sum(d_k_norm * k_hat, axis=0)), "ctx"
    )
    d_q_raw = (q_inv[:, None] * (q_scaled - q_hat * (q_inner / D)[:, None])).astype(jnp.bfloat16)
    d_k_raw = (k_inv[:, None] * (k_scaled - k_hat * (k_inner / KVD)[:, None])).astype(jnp.bfloat16)
    d_values = own_dv.reshape(local_rows, kv_heads * DH).astype(jnp.bfloat16)
    return (d_q_raw, d_k_raw, d_values, d_q_gain, d_k_gain)


def solution(mesh):
    return jax.shard_map(
        per_device,
        mesh=mesh,
        in_specs=(
            P("ctx", "tp"),
            P("ctx", "tp"),
            P("ctx", "tp"),
            P("ctx", "tp"),
            P("tp"),
            P("tp"),
            P(),
        ),
        out_specs=(P("ctx", "tp"), P("ctx", "tp"), P("ctx", "tp"), P("tp"), P("tp")),
        check_vma=False,
    )
```

profile of v0, /device:TPU:1, one launch (start us, length us, event | category | flops | bytes accessed | tf_op | source)
XLA Modules:
  0.0 338.7 jit_solution(9381182435846644304)
XLA Ops:
  10.2 13.4 %all-reduce.2 = (f32[256]{0:T(256)S(1)}, f32[256]{0:T(256)S(1)}) all-reduce(f32[256]{0:T(256)S(1)} %fusion.92, f32[256]{0:T(256)S(1)} %fusion.70), channel_id=1, replica_groups=mesh['ctx'=16,'tp'=8] {'tp'}, use_global_device_ids=true, to_apply=%region_3.4 | all-reduce | flops 512 | bytes 4096 | tf_op jit(solution)/shard_map/psum | solution.py:112
  30.4 24.4 %all-gather.6.cloned.1.call-done = bf16[4096,128]{1,0:T(8,128)(2,1)} async-done(((bf16[256,128]{1,0:T(8,128)(2,1)}), bf16[4096,128]{1,0:T(8,128)(2,1)}) %all-gather.6.cloned.1.call-update) | async-done | bytes 1048592 | tf_op jit(solution)/shard_map/all_gather | solution.py:146
  54.8 44.9 %all-gather.4.cloned.1.call-done = bf16[4096,1,128]{2,0,1:T(8,128)(2,1)} async-done(((bf16[256,1,128]{2,0,1:T(8,128)(2,1)}), bf16[4096,1,128]{2,0,1:T(8,128)(2,1)}) %all-gather.4.cloned.1.call-update) | async-done | bytes 1048592 | tf_op jit(solution)/shard_map/all_gather | solution.py:145
  99.6 33.1 %while.38 = (s32[]{:T(128)}, f32[1,5,256]{2,1,0:T(8,128)S(1)}, f32[1,5,256]{2,1,0:T(8,128)S(1)}, f32[1,5,256]{2,1,0:T(8,128)S(1)}, s32[32]{0:T(128)S(1)}, /*inde...) while((s32[]{:T(128)}, f32[1,5,256]{2,1,0:T(8,128)S(1)}, ...), condition=%wide.region_14.15_spmd, body=%wide.region_6.0_spmd.sunk | while | flops 689833728 | bytes 18075084 | solution.py:100
  101.7 6.2 %conditional.4 = (f32[1,5,256]{2,1,0:T(8,128)S(1)}, f32[1,5,256]{2,1,0:T(8,128)S(1)}, f32[1,5,256]{2,1,0:T(8,128)S(1)}) conditional(s32[]{:T(128)} %convert_element_type.147, (s32[1024]{0:T(1024)S(1)}, s32[256]{0:T(256)S(1)}, s32[]{:T(128)}, bf16[4096,1,128]{2,0,1:T(8,128)(2,1)}, bf16[256,1,5,128]{3,0,2,1:T(8,128)(2,1)S(1)}, ...), branch_computations={%region_9.12_spmd, %region_13.13_spmd} | conditional | flops 689704704 | bytes 18043970 | solution.py:83
  101.9 1.9 fusion.1
  103.9 2.7 fusion
  106.6 1.3 fusion.2
  109.9 6.2 %conditional.4 = (f32[1,5,256]{2,1,0:T(8,128)S(1)}, f32[1,5,256]{2,1,0:T(8,128)S(1)}, f32[1,5,256]{2,1,0:T(8,128)S(1)}) conditional(s32[]{:T(128)} %convert_element_type.147, (s32[1024]{0:T(1024)S(1)}, s32[256]{0:T(256)S(1)}, s32[]{:T(128)}, bf16[4096,1,128]{2,0,1:T(8,128)(2,1)}, bf16[256,1,5,128]{3,0,2,1:T(8,128)(2,1)S(1)}, ...), branch_computations={%region_9.12_spmd, %region_13.13_spmd} | conditional | flops 689704704 | bytes 18043970 | solution.py:83
  110.2 1.9 fusion.1
  112.1 2.7 fusion
  114.9 1.3 fusion.2
  118.2 6.2 %conditional.4 = (f32[1,5,256]{2,1,0:T(8,128)S(1)}, f32[1,5,256]{2,1,0:T(8,128)S(1)}, f32[1,5,256]{2,1,0:T(8,128)S(1)}) conditional(s32[]{:T(128)} %convert_element_type.147, (s32[1024]{0:T(1024)S(1)}, s32[256]{0:T(256)S(1)}, s32[]{:T(128)}, bf16[4096,1,128]{2,0,1:T(8,128)(2,1)}, bf16[256,1,5,128]{3,0,2,1:T(8,128)(2,1)S(1)}, ...), branch_computations={%region_9.12_spmd, %region_13.13_spmd} | conditional | flops 689704704 | bytes 18043970 | solution.py:83
  118.5 1.9 fusion.1
  120.4 2.7 fusion
  123.1 1.3 fusion.2
  126.5 6.2 %conditional.4 = (f32[1,5,256]{2,1,0:T(8,128)S(1)}, f32[1,5,256]{2,1,0:T(8,128)S(1)}, f32[1,5,256]{2,1,0:T(8,128)S(1)}) conditional(s32[]{:T(128)} %convert_element_type.147, (s32[1024]{0:T(1024)S(1)}, s32[256]{0:T(256)S(1)}, s32[]{:T(128)}, bf16[4096,1,128]{2,0,1:T(8,128)(2,1)}, bf16[256,1,5,128]{3,0,2,1:T(8,128)(2,1)S(1)}, ...), branch_computations={%region_9.12_spmd, %region_13.13_spmd} | conditional | flops 689704704 | bytes 18043970 | solution.py:83
  126.7 1.9 fusion.1
  128.7 2.7 fusion
  133.7 1.4 broadcast.433
  135.1 44.8 %while.39 = (s32[]{:T(128)}, f32[256,1,5,128]{0,3,2,1:T(8,128)S(1)}, f32[4096,1,128]{2,0,1:T(8,128)}, f32[4096,1,128]{2,0,1:T(8,128)S(1)}, s32[32]{0:T(128)S(1)}...) while((s32[]{:T(128)}, ...), condition=%wide.region_20.21_spmd, body=%wide.region_15.20_spmd.sunk | while | flops 1691678720 | bytes 30232148 | solution.py:100
  137.2 9.1 %conditional.5 = ((f32[256,1,5,128]{0,3,2,1:T(8,128)S(1)}, f32[4096,1,128]{2,0,1:T(8,128)}, f32[4096,1,128]{2,0,1:T(8,128)S(1)})) conditional(s32[]{:T(128)} %convert_element_type.148, (s32[]{:T(128)}, bf16[4096,1,128]{2,0,1:T(8,128)(2,1)}, s32[1024]{0:T(1024)S(1)}, s32[256]{0:T(256)S(1)}, bf16[256,1,5,128]{3,0,2,1:T(8,128)(2,1)S(1)}, ...), branch_computations={%region_18.18_spmd, %region_19.19_spmd} | conditional | flops 1691549696 | bytes 30211242 | solution.py:83
  137.5 1.8 fusion.42
  139.3 2.6 fusion.24
  143.0 1.6 fusion.38
  144.6 1.7 fusion.37
  148.4 9.1 %conditional.5 = ((f32[256,1,5,128]{0,3,2,1:T(8,128)S(1)}, f32[4096,1,128]{2,0,1:T(8,128)}, f32[4096,1,128]{2,0,1:T(8,128)S(1)})) conditional(s32[]{:T(128)} %convert_element_type.148, (s32[]{:T(128)}, bf16[4096,1,128]{2,0,1:T(8,128)(2,1)}, s32[1024]{0:T(1024)S(1)}, s32[256]{0:T(256)S(1)}, bf16[256,1,5,128]{3,0,2,1:T(8,128)(2,1)S(1)}, ...), branch_computations={%region_18.18_spmd, %region_19.19_spmd} | conditional | flops 1691549696 | bytes 30211242 | solution.py:83
  148.7 1.8 fusion.42
  150.5 2.6 fusion.24
  154.2 1.6 fusion.38
  155.8 1.7 fusion.37
  159.6 9.0 %conditional.5 = ((f32[256,1,5,128]{0,3,2,1:T(8,128)S(1)}, f32[4096,1,128]{2,0,1:T(8,128)}, f32[4096,1,128]{2,0,1:T(8,128)S(1)})) conditional(s32[]{:T(128)} %convert_element_type.148, (s32[]{:T(128)}, bf16[4096,1,128]{2,0,1:T(8,128)(2,1)}, s32[1024]{0:T(1024)S(1)}, s32[256]{0:T(256)S(1)}, bf16[256,1,5,128]{3,0,2,1:T(8,128)(2,1)S(1)}, ...), branch_computations={%region_18.18_spmd, %region_19.19_spmd} | conditional | flops 1691549696 | bytes 30211242 | solution.py:83
  159.9 1.8 fusion.42
  161.7 2.6 fusion.24
  165.4 1.6 fusion.38
  167.0 1.6 fusion.37
  170.8 9.1 %conditional.5 = ((f32[256,1,5,128]{0,3,2,1:T(8,128)S(1)}, f32[4096,1,128]{2,0,1:T(8,128)}, f32[4096,1,128]{2,0,1:T(8,128)S(1)})) conditional(s32[]{:T(128)} %convert_element_type.148, (s32[]{:T(128)}, bf16[4096,1,128]{2,0,1:T(8,128)(2,1)}, s32[1024]{0:T(1024)S(1)}, s32[256]{0:T(256)S(1)}, bf16[256,1,5,128]{3,0,2,1:T(8,128)(2,1)S(1)}, ...), branch_computations={%region_18.18_spmd, %region_19.19_spmd} | conditional | flops 1691549696 | bytes 30211242 | solution.py:83
  171.1 1.8 fusion.42
  172.9 2.6 fusion.24
  176.6 1.6 fusion.38
  178.2 1.7 fusion.37
  181.7 71.9 %reduce-scatter.3.cloned.1.call-done = f32[256,1,128]{2,0,1:T(8,128)} async-done(((f32[4096,1,128]{2,0,1:T(8,128)}), f32[256,1,128]{2,0,1:T(8,128)}) %reduce-scatter.3.cloned.1.call-update) | async-done | bytes 131088 | tf_op jit(solution)/shard_map/reduce_scatter | solution.py:184
  253.6 1.5 fusion.93
  256.1 14.1 %all-reduce.1 = (f32[256]{0:T(256)S(1)}, f32[256]{0:T(256)S(1)}) all-reduce(f32[256]{0:T(256)S(1)} %get-tuple-element.940, f32[256]{0:T(256)S(1)} %get-tuple-element.942), channel_id=1, replica_groups=mesh['ctx'=16,'tp'=8] {'tp'}, use_global_device_ids=true, to_apply=%region_22.23 | all-reduce | flops 512 | bytes 4096 | tf_op jit(solution)/shard_map/psum | solution.py:193
  271.9 32.7 %all-reduce = (f32[640]{0:T(1024)}, f32[128]{0:T(128)}) all-reduce(f32[640]{0:T(1024)S(1)} %get-tuple-element.939, f32[128]{0:T(128)S(1)} %get-tuple-element.941), channel_id=1, replica_groups=mesh['ctx'=16,'tp'=8] {'ctx'}, use_global_device_ids=true, to_apply=%region_28.29 | all-reduce | flops 768 | bytes 6144 | tf_op jit(solution)/shard_map/psum | solution.py:196
  304.7 1.5 fusion.90
  306.1 24.5 %reduce-scatter.5.cloned.1.call-done = f32[256,1,128]{2,0,1:T(8,128)} async-done(((f32[4096,1,128]{2,0,1:T(8,128)}), f32[256,1,128]{2,0,1:T(8,128)}) %reduce-scatter.5.cloned.1.call-update) | async-done | bytes 131088 | tf_op jit(solution)/shard_map/reduce_scatter | solution.py:185
  330.6 1.5 convert_bitcast_fusion
  (134 shorter events, 28.5 us)
Async XLA Ops:
  7.2 92.5 %copy-start.4 = (s32[32]{0:T(128)S(1)}, s32[32]{0:T(128)}, u32[]{:S(2)}) copy-start(s32[32]{0:T(128)} %param.21) | copy-start | bytes 388
  7.2 47.6 %all-gather.6.cloned.1.call-start = ((), (), s32[]{:S(2)}) async-start(), calls=%async_computation.5 | async-start | bytes 1114112 | tf_op jit(solution)/shard_map/all_gather | solution.py:146
  7.9 91.7 %all-gather.4.cloned.1.call-start = ((), (), s32[]{:S(2)}) async-start(), calls=%async_computation.2 | async-start | bytes 1114112 | tf_op jit(solution)/shard_map/all_gather | solution.py:145
  23.6 5.8 %copy-start.12 = (f32[64]{0:T(128)}, f32[64]{0:T(128)S(1)}, u32[]{:S(2)}) copy-start(f32[64]{0:T(128)S(1)} %multiply_power_fusion) | copy-start | bytes 772
  24.4 1.0 copy-start.6
  24.4 5.0 %copy-start.8 = (f32[256]{0:T(256)}, f32[256]{0:T(256)S(1)}, u32[]{:S(2)}) copy-start(f32[256]{0:T(256)S(1)} %get-tuple-element.1021) | copy-start | bytes 3076
  26.7 226.9 %reduce-scatter.3.cloned.1.call-start = ((), (), s32[]{:S(2)}) async-start(), calls=%async_computation.3 | async-start | bytes 2228224 | tf_op jit(solution)/shard_map/reduce_scatter | solution.py:184
  132.7 0.7 copy-start.2
  137.3 2.1 copy-start.3
  137.3 2.1 copy-start.10
  137.3 2.1 copy-start.11
  148.4 2.1 copy-start.3
  148.5 2.1 copy-start.10
  148.5 2.1 copy-start.11
  159.6 2.1 copy-start.3
  159.7 2.1 copy-start.10
  159.7 2.1 copy-start.11
  170.8 2.1 copy-start.3
  170.8 2.1 copy-start.10
  170.8 2.1 copy-start.11
  179.9 1.4 copy-start
  179.9 1.5 copy-start.5
  179.9 1.5 copy-start.9
  179.9 75.3 %copy-start.1 = (bf16[256,128]{1,0:T(8,128)(2,1)S(1)}, bf16[256,128]{1,0:T(8,128)(2,1)}, u32[]{:S(2)}) copy-start(bf16[256,128]{1,0:T(8,128)(2,1)} %param.16) | copy-start | bytes 196612
  179.9 75.3 %copy-start.7 = (f32[256]{0:T(256)S(1)}, f32[256]{0:T(256)}, u32[]{:S(2)}) copy-start(f32[256]{0:T(256)} %copy-done.6) | copy-start | bytes 3076
  179.9 150.7 %reduce-scatter.5.cloned.1.call-start = ((), (), s32[]{:S(2)}) async-start(), calls=%async_computation.4 | async-start | bytes 2228224 | tf_op jit(solution)/shard_map/reduce_scatter | solution.py:185
Sparse Core Ops, SparseCore 0:
  10.2 44.5 all-gather.5
  57.5 42.0 all-gather.3
  180.0 73.5 reduce-scatter.2
  257.1 73.4 reduce-scatter.4
where the time goes:
time: 341 us; the launch traced here: 339 us
  waiting for transfers between devices  166 us (49%)
  blocking collectives  60.3 us (18%)
  matrix products  53.5 us (16%)
  other arithmetic  26.4 us (8%)
  between operations  14 us (4%)
  loops' own time  11.2 us (3%)
  local copies, waits for them, and re-layouts  6.7 us (2%)
    reduce_scatter x1, waiting for transfers between devices, per_device(): lax.psum_scatter(gradients[1], 'ctx', scatter_dimension=0, tiled=True)  71.9 us
    all_gather x1, waiting for transfers between devices, per_device(): lax.all_gather(k_rot, 'ctx', axis=0, tiled=True)  44.9 us
    psum x1, blocking collectives, per_device(): lax.psum((jnp.sum(d_q_norm * q_hat, axis=0), jnp.sum(d_k_norm * k_hat, ax...  32.7 us
    reduce_scatter x1, waiting for transfers between devices, per_device(): lax.psum_scatter(gradients[2], 'ctx', scatter_dimension=0, tiled=True)  24.5 us
    all_gather x1, waiting for transfers between devices, per_device(): lax.all_gather(v_heads, 'ctx', axis=0, tiled=True)  24.4 us
    dot_general x8, matrix products, tile_scores(): jnp.einsum('rkgd,nkd->kgrn', queries, key_rows, preferred_element_type=jn...  15 us
    psum x1, blocking collectives, per_device(): lax.psum((jnp.sum(q_scaled * q_hat, axis=1), jnp.sum(k_scaled * k_hat, ax...  14.1 us
    psum x1, blocking collectives, per_device(): lax.psum((jnp.sum(q_float * q_float, axis=1), jnp.sum(k_float * k_float,...  13.4 us
  transfers between devices with their start and end apart: 4, of which 4 were waited for; matrix products, arithmetic and copies ran while one was open for 4% of the time, Pallas kernels for 0%

commit v1 on v0

v1 whole, which is shorter than its diff:
```python
import functools
import math

import jax
import jax.numpy as jnp
import numpy as np
from jax import lax
from jax.experimental import pallas as pl
from jax.experimental.pallas import tpu as pltpu
from jax.sharding import PartitionSpec as P

D = 5120
KVD = 1024
DH = 128
SPAN = 128
SPANS = 32
GROUP = 5
QW = GROUP * DH
EPS = 1e-06
THETA = 500000.0
NEG = -1e30
SCALE = DH ** (-0.5)
C2 = SCALE * math.log2(math.e)
RING = 4
SLOTS = 16
F32 = jnp.float32
BF16 = jnp.bfloat16

ORDER = [
    (0, 0), (0, 3), (3, 0), (0, 1), (1, 0), (3, 3), (1, 3), (3, 1),
    (1, 1), (0, 2), (2, 0), (3, 2), (2, 3), (1, 2), (2, 1), (2, 2),
]
SLOT = {pair: number for number, pair in enumerate(ORDER)}
CHUNKS = ((0, 256), (256, 256), (512, 128))
LOW, HIGH = 0, 1
KEY, VAL = 0, 1


def primary_view(half, slot):
    oz, ox = ORDER[slot]
    return (ox, oz) if half == LOW else (oz, ox)


def slot_of(half, first, second):
    return SLOT[(second, first)] if half == LOW else SLOT[(first, second)]


def gather_sends(half, slot):
    first, second = primary_view(half, slot)
    sends = []
    if second == 0:
        if first == 0:
            sends += [(0, 1, slot_of(half, 3, 0)), (0, 3, slot_of(half, 1, 0))]
        if first == 3:
            sends += [(0, 1, slot_of(half, 2, 0))]
        sends += [(1, 1, slot_of(half, first, 3)), (1, 3, slot_of(half, first, 1))]
    if second == 3:
        sends += [(1, 1, slot_of(half, first, 2))]
    return sends


def tables():
    freq = np.asarray(
        np.float32(THETA) ** (-np.arange(DH // 2, dtype=np.float32) / np.float32(DH // 2)),
        np.float64,
    )
    sign = np.concatenate([-np.ones(DH // 2), np.ones(DH // 2)])

    def pair(numbers):
        angle = np.asarray(numbers, np.float64)[:, None] * freq[None, :]
        cos = np.concatenate([np.cos(angle)] * 2, axis=1)
        sin = np.concatenate([np.sin(angle)] * 2, axis=1) * sign
        return cos, sin

    cos_t, sin_t = pair(np.arange(SPAN))
    cos_s, sin_s = pair(np.arange(SPANS) * SPAN)
    token = np.stack([cos_t, sin_t]).astype(np.float32)
    span = np.stack([cos_s, sin_s])[:, :, None, :].astype(np.float32)
    return jnp.asarray(token), jnp.asarray(span)


def kernel(
    so_ref, q_ref, k_ref, v_ref, do_ref, qg_ref, kg_ref, tab_ref, span_ref,
    dq_out, dk_out, dv_out, dqg_out, dkg_out,
    sel_ref, kv, qs, qt, dos, dot_, rope, qi, ki,
    e_a, e_b, dp_a, dp_b, mh, lh, dh, ml, ll, dl, fh, fl, delta,
    pb, dsb, acc, cb, stage, gotr, pstage, gotp, sg, dkn,
    stat, gain_buf,
    ag_ssem, ag_rsem, rs_ssem, rs_rsem, ps_ssem, ps_rsem,
    st_ssem, st_rsem, gn_ssem, gn_rsem,
):
    ctx = lax.axis_index("ctx")
    tp = lax.axis_index("tp")
    z, x = ctx // RING, ctx % RING
    flip = tp % 2

    def at_offset(oz, ox):
        nz = (z + jnp.where(flip == 0, oz, RING - oz)) % RING
        nx = (x + jnp.where(flip == 0, ox, RING - ox)) % RING
        return nz * RING + nx

    def tp_peer(offset):
        return (tp + offset) % 8

    barrier = pltpu.get_barrier_semaphore()
    for slot in range(1, SLOTS):
        pl.semaphore_signal(
            barrier, inc=1, device_id={"ctx": at_offset(*ORDER[slot])},
            device_id_type=pl.DeviceIdType.MESH,
        )
    for offset in range(1, 8):
        pl.semaphore_signal(
            barrier, inc=1, device_id={"tp": tp_peer(offset)},
            device_id_type=pl.DeviceIdType.MESH,
        )

    s0, s1 = so_ref[2 * ctx], so_ref[2 * ctx + 1]
    low = jnp.minimum(s0, s1)
    spans = (low, SPANS - 1 - low)
    offs = (jnp.where(s0 < s1, 0, 1), jnp.where(s0 < s1, 1, 0))
    for slot in range(1, SLOTS):
        other = at_offset(*ORDER[slot])
        a = jnp.minimum(so_ref[2 * other], so_ref[2 * other + 1])
        sel_ref[slot] = jnp.where(a < low, 1, 0)

    for half in (LOW, HIGH):
        kv[VAL, half, 0] = v_ref[offs[half]]

    pl.semaphore_wait(barrier, 22)

    axis_of = {LOW: ("x", "z"), HIGH: ("z", "x")}

    def neighbour(half, axis, step):
        name = axis_of[half][axis]
        return at_offset(step, 0) if name == "z" else at_offset(0, step)

    def gather_copy(which, half, slot, axis, step, dst):
        return pltpu.make_async_remote_copy(
            src_ref=kv.at[which, half, slot],
            dst_ref=kv.at[which, half, dst],
            send_sem=ag_ssem.at[which, half, dst],
            recv_sem=ag_rsem.at[which, half, dst],
            device_id={"ctx": neighbour(half, axis, step)},
            device_id_type=pl.DeviceIdType.MESH,
        )

    def gather_wait(which, half, slot):
        gather_copy(which, half, slot, 0, 1, slot).wait_recv()

    def gather_forward(which, half, slot):
        for axis, step, dst in gather_sends(half, slot):
            gather_copy(which, half, slot, axis, step, dst).start()

    def hop(which, slots):
        for slot in slots:
            for half in (LOW, HIGH):
                gather_wait(which, half, slot)
                gather_forward(which, half, slot)

    gather_forward(VAL, LOW, 0)
    gather_forward(VAL, HIGH, 0)

    def stat_copy(kind, offset):
        return pltpu.make_async_remote_copy(
            src_ref=stat.at[kind, 0],
            dst_ref=stat.at[kind, offset],
            send_sem=st_ssem.at[kind, offset],
            recv_sem=st_rsem.at[kind, offset],
            device_id={"tp": tp_peer(offset)},
            device_id_type=pl.DeviceIdType.MESH,
        )

    def stat_send(kind):
        for offset in range(1, 8):
            stat_copy(kind, offset).start()

    def stat_total(kind):
        total = stat[kind, 0]
        for offset in range(1, 8):
            stat_copy(kind, offset).wait_recv()
            total = total + stat[kind, offset]
        return total

    def token_sums(square):
        return jnp.sum(jnp.transpose(square), axis=0, keepdims=True)

    def spread(row):
        return jnp.transpose(jnp.broadcast_to(row, (SPAN, SPAN)))

    def head(number):
        return slice(number * DH, (number + 1) * DH)

    stat[0, 0] = jnp.zeros((8, 2 * SPAN), F32)
    for half in (LOW, HIGH):
        square = jnp.zeros((SPAN, DH), F32)
        for h in range(GROUP):
            part = q_ref[offs[half], :, head(h)].astype(F32)
            square = square + part * part
        stat[0, 0, 0:1, half * SPAN:(half + 1) * SPAN] = token_sums(square)
        part = k_ref[offs[half]].astype(F32)
        stat[0, 0, 1:2, half * SPAN:(half + 1) * SPAN] = token_sums(part * part)
    stat_send(0)

    cos_t, sin_t = tab_ref[0], tab_ref[1]
    for half in (LOW, HIGH):
        cos_s = span_ref[0, spans[half]]
        sin_s = span_ref[1, spans[half]]
        rope[half, 0] = cos_s * cos_t - sin_s * sin_t
        rope[half, 1] = sin_s * cos_t + cos_s * sin_t
    for half in (LOW, HIGH):
        for h in range(GROUP):
            part = do_ref[offs[half], :, head(h)]
            dos[half, head(h), :] = part
            dot_[half, :, head(h)] = jnp.transpose(part)

    def rotated(half, part, sign):
        turned = pltpu.roll(part, DH // 2, 1) * rope[half, 1]
        straight = part * rope[half, 0]
        return straight + turned if sign > 0 else straight - turned

    total = stat_total(0)
    q_inv = lax.rsqrt(total[0:1, :] / D + EPS)
    k_inv = lax.rsqrt(total[1:2, :] / KVD + EPS)
    for half in (LOW, HIGH):
        ki[half] = spread(k_inv[:, half * SPAN:(half + 1) * SPAN])
        part = k_ref[offs[half]].astype(F32)
        part = part * ki[half] * kg_ref[...]
        kv[KEY, half, 0] = rotated(half, part, 1).astype(BF16)
        gather_forward(KEY, half, 0)

    hop(VAL, (1, 2, 3, 4))

    for half in (LOW, HIGH):
        qi[half] = spread(q_inv[:, half * SPAN:(half + 1) * SPAN])
        for h in range(GROUP):
            part = q_ref[offs[half], :, head(h)].astype(F32)
            part = part * qi[half] * qg_ref[:, head(h)]
            turned = rotated(half, part, 1).astype(BF16)
            qs[half, head(h), :] = turned
            qt[half, :, head(h)] = jnp.transpose(turned)

    hop(VAL, (5, 6, 7, 8, 9, 10))

    def mm(a, b):
        return jnp.dot(a, b, preferred_element_type=F32)

    def pick(is_low, which, slot):
        return jnp.where(is_low, kv[which, LOW, slot], kv[which, HIGH, slot])

    def values_pass(slot):
        is_low = sel_ref[slot] == 1
        other = 1 - sel_ref[slot]
        v_low, v_other = kv[VAL, LOW, slot], pick(is_low, VAL, slot)
        for start, width in CHUNKS:
            cols = pl.ds(start, width)
            dp_a[slot, :, cols] = mm(v_low, dot_[HIGH, :, cols])
            dp_b[slot, :, cols] = mm(v_other, dot_[other, :, cols])

    def scores(keys, half, cols, d_probs, exps, slot, mask=None):
        s = mm(keys, qt[half, :, cols])
        if mask is not None:
            s = jnp.where(mask, s, NEG)
        top = jnp.max(s, axis=0, keepdims=True)
        e = jnp.exp2(s * C2 - top * C2)
        exps[slot, :, cols] = e
        return (
            top,
            jnp.sum(e, axis=0, keepdims=True),
            jnp.sum(e * d_probs[slot, :, cols], axis=0, keepdims=True),
        )

    def put(tabs, row, cols, stats):
        for tab, value in zip(tabs, stats):
            tab[row, :, cols] = value

    tabs_high, tabs_low = (mh, lh, dh), (ml, ll, dl)

    def keys_pass(slot):
        chosen = sel_ref[slot]
        is_low = chosen == 1
        k_low, k_other = kv[KEY, LOW, slot], pick(is_low, KEY, slot)
        for start, width in CHUNKS:
            cols = pl.ds(start, width)
            put(tabs_high, slot, cols, scores(k_low, HIGH, cols, dp_a, e_a, slot))
            top, total, dots = scores(k_other, 1 - chosen, cols, dp_b, e_b, slot)
            put(tabs_high, slot + 15, cols, (jnp.where(is_low, NEG, top), total, dots))
            put(tabs_low, slot, cols, (jnp.where(is_low, top, NEG), total, dots))

    def own_values():
        for start, width in CHUNKS:
            cols = pl.ds(start, width)
            dp_a[0, :, cols] = mm(kv[VAL, LOW, 0], dot_[HIGH, :, cols])
            dp_b[0, :, cols] = mm(kv[VAL, LOW, 0], dot_[LOW, :, cols])
            dp_b[16, :, cols] = mm(kv[VAL, HIGH, 0], dot_[HIGH, :, cols])

    def own_keys():
        for start, width in CHUNKS:
            cols = pl.ds(start, width)
            shape = (SPAN, width)
            mask = lax.broadcasted_iota(jnp.int32, shape, 0) <= (
                lax.broadcasted_iota(jnp.int32, shape, 1) % SPAN
            )
            put(tabs_high, 0, cols, scores(kv[KEY, LOW, 0], HIGH, cols, dp_a, e_a, 0))
            put(tabs_low, 0, cols, scores(kv[KEY, LOW, 0], LOW, cols, dp_b, e_b, 0, mask))
            put(tabs_high, 31, cols, scores(kv[KEY, HIGH, 0], HIGH, cols, dp_b, e_b, 16, mask))

    own_values()
    lax.fori_loop(1, 9, lambda slot, _: (values_pass(slot), 0)[1], 0)
    hop(KEY, (1, 2, 3, 4))
    own_keys()
    hop(VAL, (11, 12, 13, 14, 15))
    hop(KEY, (5, 6, 7, 8, 9, 10))
    lax.fori_loop(9, 16, lambda slot, _: (values_pass(slot), 0)[1], 0)
    lax.fori_loop(1, 11, lambda slot, _: (keys_pass(slot), 0)[1], 0)
    hop(KEY, (11, 12, 13, 14, 15))
    lax.fori_loop(11, 16, lambda slot, _: (keys_pass(slot), 0)[1], 0)

    def finish(tabs, factors, half):
        tops, sums, dots = (tab[...] for tab in tabs)
        weights = jnp.exp2((tops - jnp.max(tops, axis=0, keepdims=True)) * C2)
        scale = 1.0 / jnp.sum(weights * sums, axis=0, keepdims=True)
        delta[half] = (jnp.sum(weights * dots, axis=0, keepdims=True) * scale)[0]
        factors[...] = weights * scale

    finish(tabs_high, fh, HIGH)
    finish(tabs_low, fl, LOW)

    def grads(exps, d_probs, slot, factor, shift, where):
        for start, width in CHUNKS:
            cols = pl.ds(start, width)
            probs = exps[slot, :, cols] * factor(cols)
            d_scores = probs * (d_probs[slot, :, cols] - shift(cols))
            pb[where, :, cols] = probs.astype(BF16)
            dsb[pl.ds(where * SPAN, SPAN), cols] = d_scores.astype(BF16)

    def rows(where):
        return pl.ds(where * SPAN, SPAN)

    def second_pass(slot):
        chosen = sel_ref[slot]
        is_low = chosen == 1
        other = 1 - chosen
        grads(e_a, dp_a, slot, lambda c: fh[slot, :, c], lambda c: delta[HIGH, :, c], 0)
        grads(
            e_b, dp_b, slot,
            lambda c: fl[slot, :, c] + fh[slot + 15, :, c],
            lambda c: delta[other, :, c], 1,
        )
        for kind, left in ((0, None), (1, None)):
            a_rows = pb[0] if kind == 0 else dsb[rows(0), :]
            b_rows = pb[1] if kind == 0 else dsb[rows(1), :]
            source = dos if kind == 0 else qs
            from_a = mm(a_rows, source[HIGH])
            from_b = mm(b_rows, source[other])
            cb[slot, LOW, kind] = from_a + jnp.where(is_low, from_b, 0.0)
            cb[slot, HIGH, kind] = jnp.where(is_low, 0.0, from_b)
        turned_low = jnp.transpose(kv[KEY, LOW, slot])
        turned_other = jnp.transpose(pick(is_low, KEY, slot))
        none = jnp.zeros_like(turned_other)
        both = jnp.concatenate([turned_low, jnp.where(is_low, none, turned_other)], axis=1)
        only_low = jnp.where(is_low, turned_other, none)
        for start, width in CHUNKS:
            cols = pl.ds(start, width)
            acc[HIGH, :, cols] += mm(both, dsb[0:2 * SPAN, cols])
            acc[LOW, :, cols] += mm(only_low, dsb[rows(1), cols])

    def own_second():
        grads(e_a, dp_a, 0, lambda c: fh[0, :, c], lambda c: delta[HIGH, :, c], 0)
        grads(e_b, dp_b, 16, lambda c: fh[31, :, c], lambda c: delta[HIGH, :, c], 1)
        grads(e_b, dp_b, 0, lambda c: fl[0, :, c], lambda c: delta[LOW, :, c], 2)
        for kind in (0, 1):
            source = dos if kind == 0 else qs
            parts = [pb[i] if kind == 0 else dsb[rows(i), :] for i in range(3)]
            cb[0, LOW, kind] = mm(parts[0], source[HIGH]) + mm(parts[2], source[LOW])
            cb[0, HIGH, kind] = mm(parts[1], source[HIGH])
        turned_low = jnp.transpose(kv[KEY, LOW, 0])
        turned_high = jnp.transpose(kv[KEY, HIGH, 0])
        both = jnp.concatenate([turned_low, turned_high], axis=1)
        for start, width in CHUNKS:
            cols = pl.ds(start, width)
            acc[HIGH, :, cols] += mm(both, dsb[0:2 * SPAN, cols])
            acc[LOW, :, cols] += mm(turned_low, dsb[rows(2), cols])

    acc[...] = jnp.zeros_like(acc)

    FAR, PLUS, MINUS = 0, 1, 2

    def ring_copy(half, first, what):
        step = 3 if what == MINUS else 1
        return pltpu.make_async_remote_copy(
            src_ref=stage.at[half, first, what],
            dst_ref=gotr.at[half, first, what],
            send_sem=rs_ssem.at[half, first, what],
            recv_sem=rs_rsem.at[half, first, what],
            device_id={"ctx": neighbour(half, 1, step)},
            device_id_type=pl.DeviceIdType.MESH,
        )

    def last_copy(half, what):
        step = 3 if what == MINUS else 1
        return pltpu.make_async_remote_copy(
            src_ref=pstage.at[half, what],
            dst_ref=gotp.at[half, what],
            send_sem=ps_ssem.at[half, what],
            recv_sem=ps_rsem.at[half, what],
            device_id={"ctx": neighbour(half, 0, step)},
            device_id_type=pl.DeviceIdType.MESH,
        )

    def send_far(half, first):
        stage[half, first, FAR] = cb[slot_of(half, first, 2), half].astype(BF16)
        ring_copy(half, first, FAR).start()

    def send_minus(half, first):
        stage[half, first, MINUS] = cb[slot_of(half, first, 3), half].astype(BF16)
        ring_copy(half, first, MINUS).start()

    def send_plus(half, first):
        ring_copy(half, first, FAR).wait_recv()
        mixed = cb[slot_of(half, first, 1), half] + gotr[half, first, FAR].astype(F32)
        stage[half, first, PLUS] = mixed.astype(BF16)
        ring_copy(half, first, PLUS).start()

    def ring_sum(half, first):
        ring_copy(half, first, PLUS).wait_recv()
        ring_copy(half, first, MINUS).wait_recv()
        return (
            cb[slot_of(half, first, 0), half]
            + gotr[half, first, PLUS].astype(F32)
            + gotr[half, first, MINUS].astype(F32)
        )

    def last_send(half, what):
        first = {FAR: 2, PLUS: 1, MINUS: 3}[what]
        total = ring_sum(half, first)
        if what == PLUS:
            last_copy(half, FAR).wait_recv()
            total = total + gotp[half, FAR].astype(F32)
        pstage[half, what] = total.astype(BF16)
        last_copy(half, what).start()

    def last_sum(half):
        total = ring_sum(half, 0)
        last_copy(half, PLUS).wait_recv()
        last_copy(half, MINUS).wait_recv()
        return total + gotp[half, PLUS].astype(F32) + gotp[half, MINUS].astype(F32)

    events = {slot: [] for slot in range(SLOTS)}
    for slot in range(1, SLOTS):
        for half in (LOW, HIGH):
            first, second = primary_view(half, slot)
            if second == 2:
                events[slot].append((send_far, half, first))
            if second == 3:
                events[slot].append((send_minus, half, first))
            if second == 1:
                events[max(slot - 2, 1)].append((send_plus, half, first))
    for half in (LOW, HIGH):
        events[4].append((last_send, half, FAR))

    def run_events(slot):
        for action, half, argument in events[slot]:
            action(half, argument)

    def second_step(number, carry):
        slot = SLOTS - 1 - number
        second_pass(slot)
        for which in range(1, SLOTS):
            if events[which]:
                pl.when(slot == which)(functools.partial(run_events, which))
        return carry

    lax.fori_loop(0, SLOTS - 1, second_step, 0)
    own_second()
    for what in (PLUS, MINUS):
        for half in (LOW, HIGH):
            last_send(half, what)

    stat[1, 0] = jnp.zeros((8, 2 * SPAN), F32)
    gain_buf[0] = jnp.zeros((8, DH), F32)
    for half in (LOW, HIGH):
        inner = jnp.zeros((SPAN, DH), F32)
        for h in range(GROUP):
            d_rot = jnp.transpose(acc[half, :, head(h)]) * SCALE
            d_norm = rotated(half, d_rot, -1)
            q_hat = q_ref[offs[half], :, head(h)].astype(F32) * qi[half]
            gain_buf[0, h:h + 1, :] += jnp.sum(d_norm * q_hat, axis=0, keepdims=True)
            scaled = d_norm * qg_ref[:, head(h)]
            sg[half, :, head(h)] = scaled
            inner = inner + scaled * q_hat
        stat[1, 0, 0:1, half * SPAN:(half + 1) * SPAN] = token_sums(inner)
    stat_send(1)

    stat[2, 0] = jnp.zeros((8, 2 * SPAN), F32)
    for half in (LOW, HIGH):
        summed = last_sum(half)
        dkn[1, half] = summed[0]
        d_norm = rotated(half, summed[1] * SCALE, -1)
        k_hat = k_ref[offs[half]].astype(F32) * ki[half]
        gain_buf[0, 5:6, :] += jnp.sum(d_norm * k_hat, axis=0, keepdims=True)
        scaled = d_norm * kg_ref[...]
        dkn[0, half] = scaled
        stat[2, 0, 0:1, half * SPAN:(half + 1) * SPAN] = token_sums(scaled * k_hat)
    stat_send(2)

    def gain_copy(slot):
        return pltpu.make_async_remote_copy(
            src_ref=gain_buf.at[0],
            dst_ref=gain_buf.at[slot],
            send_sem=gn_ssem.at[slot],
            recv_sem=gn_rsem.at[slot],
            device_id={"ctx": at_offset(*ORDER[slot])},
            device_id_type=pl.DeviceIdType.MESH,
        )

    for slot in range(1, SLOTS):
        gain_copy(slot).start()

    q_inner = stat_total(1)[0:1, :] / D
    for half in (LOW, HIGH):
        inner = spread(q_inner[:, half * SPAN:(half + 1) * SPAN])
        for h in range(GROUP):
            q_hat = q_ref[offs[half], :, head(h)].astype(F32) * qi[half]
            sg[half, :, head(h)] = qi[half] * (sg[half, :, head(h)] - q_hat * inner)

    first_half = jnp.where(s0 < s1, LOW, HIGH)
    for place, half in ((0, first_half), (1, 1 - first_half)):
        dq_out[place * SPAN:(place + 1) * SPAN, :] = sg[half].astype(BF16)
        dv_out[place * SPAN:(place + 1) * SPAN, :] = dkn[1, half].astype(BF16)

    k_inner = stat_total(2)[0:1, :] / KVD
    for half in (LOW, HIGH):
        inner = spread(k_inner[:, half * SPAN:(half + 1) * SPAN])
        k_hat = k_ref[offs[half]].astype(F32) * ki[half]
        dkn[0, half] = ki[half] * (dkn[0, half] - k_hat * inner)
    for place, half in ((0, first_half), (1, 1 - first_half)):
        dk_out[place * SPAN:(place + 1) * SPAN, :] = dkn[0, half].astype(BF16)

    total = gain_buf[0]
    for slot in range(1, SLOTS):
        gain_copy(slot).wait_recv()
        total = total + gain_buf[slot]
    for h in range(GROUP):
        dqg_out[:, head(h)] = total[h:h + 1, :]
    dkg_out[...] = total[5:6, :]

    for which in (KEY, VAL):
        for half in (LOW, HIGH):
            for slot in range(SLOTS):
                for axis, step, dst in gather_sends(half, slot):
                    gather_copy(which, half, slot, axis, step, dst).wait_send()
    for half in (LOW, HIGH):
        for what in (FAR, PLUS, MINUS):
            for first in range(RING):
                ring_copy(half, first, what).wait_send()
            last_copy(half, what).wait_send()
    for kind in range(3):
        for offset in range(1, 8):
            stat_copy(kind, offset).wait_send()
    for slot in range(1, SLOTS):
        gain_copy(slot).wait_send()


def per_device(q_raw, k_raw, values, d_out, q_gain, k_gain, span_order):
    token_table, span_table = tables()
    vmem = pl.BlockSpec(memory_space=pltpu.VMEM)
    smem = pl.BlockSpec(memory_space=pltpu.SMEM)
    tile = (SPAN, DH)
    dma = pltpu.SemaphoreType.DMA
    wide = (SPAN, QW)
    scratch = [
        pltpu.SMEM((SLOTS,), jnp.int32),
        pltpu.VMEM((2, 2, SLOTS) + tile, BF16),
        pltpu.VMEM((2, QW, DH), BF16),
        pltpu.VMEM((2, DH, QW), BF16),
        pltpu.VMEM((2, QW, DH), BF16),
        pltpu.VMEM((2, DH, QW), BF16),
        pltpu.VMEM((2, 2) + tile, F32),
        pltpu.VMEM((2,) + tile, F32),
        pltpu.VMEM((2,) + tile, F32),
        pltpu.VMEM((16,) + wide, F32),
        pltpu.VMEM((17,) + wide, F32),
        pltpu.VMEM((16,) + wide, F32),
        pltpu.VMEM((17,) + wide, F32),
        pltpu.VMEM((32, 1, QW), F32),
        pltpu.VMEM((32, 1, QW), F32),
        pltpu.VMEM((32, 1, QW), F32),
        pltpu.VMEM((16, 1, QW), F32),
        pltpu.VMEM((16, 1, QW), F32),
        pltpu.VMEM((16, 1, QW), F32),
        pltpu.VMEM((32, 1, QW), F32),
        pltpu.VMEM((16, 1, QW), F32),
        pltpu.VMEM((2, 1, QW), F32),
        pltpu.VMEM((3,) + wide, BF16),
        pltpu.VMEM((3 * SPAN, QW), BF16),
        pltpu.VMEM((2,) + wide, F32),
        pltpu.VMEM((SLOTS, 2, 2) + tile, F32),
        pltpu.VMEM((2, RING, 3, 2) + tile, BF16),
        pltpu.VMEM((2, RING, 3, 2) + tile, BF16),
        pltpu.VMEM((2, 3, 2) + tile, BF16),
        pltpu.VMEM((2, 3, 2) + tile, BF16),
        pltpu.VMEM((2,) + wide, F32),
        pltpu.VMEM((2, 2) + tile, F32),
        pltpu.VMEM((3, 8, 8, 2 * SPAN), F32),
        pltpu.VMEM((SLOTS, 8, DH), F32),
        dma((2, 2, SLOTS)), dma((2, 2, SLOTS)),
        dma((2, RING, 3)), dma((2, RING, 3)),
        dma((2, 3)), dma((2, 3)),
        dma((3, 8)), dma((3, 8)),
        dma((SLOTS,)), dma((SLOTS,)),
    ]
    rows = 2 * SPAN
    outs = pl.pallas_call(
        kernel,
        out_shape=(
            jax.ShapeDtypeStruct((rows, QW), BF16),
            jax.ShapeDtypeStruct((rows, DH), BF16),
            jax.ShapeDtypeStruct((rows, DH), BF16),
            jax.ShapeDtypeStruct((1, QW), F32),
            jax.ShapeDtypeStruct((1, DH), F32),
        ),
        in_specs=[smem] + [vmem] * 8,
        out_specs=(vmem,) * 5,
        scratch_shapes=scratch,
        compiler_params=pltpu.CompilerParams(
            collective_id=0, has_side_effects=True, vmem_limit_bytes=56 * 2**20
        ),
    )(
        span_order,
        q_raw.reshape(2, SPAN, QW), k_raw.reshape(2, SPAN, DH),
        values.reshape(2, SPAN, DH), d_out.reshape(2, SPAN, QW),
        q_gain.reshape(1, QW), k_gain.reshape(1, DH), token_table, span_table,
    )
    return outs[0], outs[1], outs[2], outs[3].reshape(QW), outs[4].reshape(DH)


def solution(mesh):
    return jax.shard_map(
        per_device,
        mesh=mesh,
        in_specs=(
            P("ctx", "tp"),
            P("ctx", "tp"),
            P("ctx", "tp"),
            P("ctx", "tp"),
            P("tp"),
            P("tp"),
            P(),
        ),
        out_specs=(P("ctx", "tp"), P("ctx", "tp"), P("ctx", "tp"), P("tp"), P("tp")),
        check_vma=False,
    )
```

time: 341 us -> 71.3 us (0.21)
  waiting for transfers between devices: 166 us -> 0 us
  Pallas kernels: 0 us -> 63.3 us
  blocking collectives: 60.3 us -> 0 us
  matrix products: 53.5 us -> 0 us
  other arithmetic: 26.4 us -> 0.6 us
  between operations: 14 us -> 0.66 us
  loops' own time: 11.2 us -> 0 us
    reduce_scatter x2 -> x0, waiting for transfers between devices: 96.4 us -> none  [the longest x1 71.9 us: per_device(): lax.psum_scatter(gradients[1], 'ctx', scatter_dimension=0, tiled=True)]
    all_gather x2 -> x0, waiting for transfers between devices: 69.3 us -> none  [the longest x1 44.9 us: per_device(): lax.all_gather(k_rot, 'ctx', axis=0, tiled=True)]
    pallas_call x0 -> x1, Pallas kernels: none -> 63.3 us  [per_device(): pl.pallas_call(kernel, out_shape=(jax.ShapeDtypeStruct((rows, QW), BF16),...]
    psum x3 -> x0, blocking collectives: 60.3 us -> none  [the longest x1 32.7 us: per_device(): lax.psum((jnp.sum(d_q_norm * q_hat, axis=0), jnp.sum(d_k_norm * k_hat, ax...]
    dot_general x28 -> x0, matrix products: 53.5 us -> none  [the longest x8 15 us: tile_scores(): jnp.einsum('rkgd,nkd->kgrn', queries, key_rows, preferred_element_type=jn...]
    another operation x10 -> x0, loops' own time: 11.2 us -> none  [the longest x2 10.5 us: in_blocks(): return lax.fori_loop(0, total_rows // block_rows, advance, carried)]
    reduce_sum x17 -> x0, other arithmetic: 8.76 us -> none  [the longest x4 5.06 us: forward_tile(): jnp.sum(weights, axis=-1)]
    reduce_min x8 -> x0, other arithmetic: 5.44 us -> none  [when_visible(): jnp.min(key_pos) > jnp.max(query_pos)]
  transfers between devices with their start and end apart: 4 -> 0, of which waited for: 4 -> 0; matrix products, arithmetic and copies ran while one was open for 4% -> 0% of each run, Pallas kernels for 0% -> 0%
where the time goes in v1:
time: 71.3 us; the launch traced here: 70.2 us
  Pallas kernels  63.3 us (89%)
  local copies, waits for them, and re-layouts  5.7 us (8%)
    pallas_call x1, Pallas kernels, per_device(): pl.pallas_call(kernel, out_shape=(jax.ShapeDtypeStruct((rows, QW), BF16),...  63.3 us
    unnamed x14, local copies, waits for them, and re-layouts  5.12 us

profile of v1, /device:TPU:1, one launch (start us, length us, event | category | flops | bytes accessed | tf_op | source)
XLA Modules:
  0.0 70.2 jit_solution(5552896470062337134)
XLA Ops:
  0.6 0.0 copy-start.2
  0.6 0.7 copy-done.2
  1.3 0.6 reshape.38.qg_ref
  1.9 63.3 %shard_map.128 = (bf16[256,640]{1,0:T(8,128)(2,1)}, bf16[256,128]{1,0:T(8,128)(2,1)}, bf16[256,128]{1,0:T(8,128)(2,1)}, f32[1,640]{1,0:T(1,128)}, f32[1,128]{1,0:T(1,128)}) custom-call(s32[32]{0:T(128)} %so_ref.1, bf16[2,128,640]{2,1,0:T(8,128)(2,1)} %bitcast.6, bf16[2,128,128]{2,1,0:T(8,128)(2,1)} %bitcast.8, bf16[2,128,128]{2,1,0:T(8,128)(2,1)} %bitcast.9, ...), custom_call_target="tpu_custom_call" | custom-call | tf_op jit(solution)/shard_map/pallas_call | solution.py:613
  65.2 0.0 copy-start.3
  65.2 0.7 copy-done.3
  65.8 0.6 reduce
  66.5 0.0 copy-start.1
  66.5 1.8 %copy.18 = bf16[256,640]{1,0:T(8,128)(2,1)} copy(bf16[256,640]{1,0:T(8,128)(2,1)} %get-tuple-element.20) | data formatting | bytes 655360
  68.2 0.0 copy-done.1
  68.2 0.0 copy-start
  68.2 0.6 copy.19
  68.8 0.2 copy-done
  69.1 0.0 copy-start.4
  69.1 0.6 copy.20
  69.7 0.0 copy-done.4
  69.7 0.5 copy.21
Async XLA Ops:
  0.6 0.7 copy-start.2
  65.2 0.7 copy-start.3
  66.5 1.8 %copy-start.1 = (bf16[256,128]{1,0:T(8,128)(2,1)S(1)}, bf16[256,128]{1,0:T(8,128)(2,1)}, u32[]{:S(2)}) copy-start(bf16[256,128]{1,0:T(8,128)(2,1)} %get-tuple-element.21) | copy-start | bytes 196612
  68.2 0.9 %copy-start = (bf16[256,128]{1,0:T(8,128)(2,1)S(1)}, bf16[256,128]{1,0:T(8,128)(2,1)}, u32[]{:S(2)}) copy-start(bf16[256,128]{1,0:T(8,128)(2,1)} %get-tuple-element.22) | copy-start | bytes 196612
  69.1 0.6 copy-start.4

commit v2 on v1

v2 whole, which is shorter than its diff:
```python
import functools
import math

import jax
import jax.numpy as jnp
import numpy as np
from jax import lax
from jax.experimental import pallas as pl
from jax.experimental.pallas import tpu as pltpu
from jax.sharding import PartitionSpec as P

D = 5120
KVD = 1024
DH = 128
SPAN = 128
SPANS = 32
GROUP = 5
QW = GROUP * DH
EPS = 1e-06
THETA = 500000.0
NEG = -1e30
SCALE = DH ** (-0.5)
C2 = SCALE * math.log2(math.e)
RING = 4
SLOTS = 16
F32 = jnp.float32
BF16 = jnp.bfloat16

ORDER = [
    (0, 0), (0, 3), (3, 0), (0, 1), (1, 0), (0, 2), (2, 0), (3, 3),
    (1, 3), (3, 1), (1, 1), (3, 2), (2, 3), (1, 2), (2, 1), (2, 2),
]
SLOT = {pair: number for number, pair in enumerate(ORDER)}
MIRROR = [SLOT[(-oz % RING, -ox % RING)] for oz, ox in ORDER]
RINGS = [(0, 1), (0, 2), (0, 3), (1, 0), (2, 0), (3, 0)]
CHUNKS = ((0, 256), (256, 256), (512, 128))
LOW, HIGH = 0, 1
KEY, VAL = 0, 1


def primary_view(half, slot):
    oz, ox = ORDER[slot]
    return (ox, oz) if half == LOW else (oz, ox)


def slot_of(half, first, second):
    return SLOT[(second, first)] if half == LOW else SLOT[(first, second)]


def gather_sends(half, slot):
    first, second = primary_view(half, slot)
    sends = []
    if second == 0:
        if first == 0:
            sends += [(0, step, slot_of(half, -step % RING, 0)) for step in (1, 3, 2)]
        sends += [(1, step, slot_of(half, first, -step % RING)) for step in (1, 3)]
        if first == 2:
            sends += [(1, 2, slot_of(half, first, 2))]
    if second == 3 and first != 2:
        sends += [(1, 1, slot_of(half, first, 2))]
    return sends


def tables():
    freq = np.asarray(
        np.float32(THETA) ** (-np.arange(DH // 2, dtype=np.float32) / np.float32(DH // 2)),
        np.float64,
    )
    sign = np.concatenate([-np.ones(DH // 2), np.ones(DH // 2)])

    def pair(numbers):
        angle = np.asarray(numbers, np.float64)[:, None] * freq[None, :]
        cos = np.concatenate([np.cos(angle)] * 2, axis=1)
        sin = np.concatenate([np.sin(angle)] * 2, axis=1) * sign
        return cos, sin

    cos_t, sin_t = pair(np.arange(SPAN))
    cos_s, sin_s = pair(np.arange(SPANS) * SPAN)
    token = np.stack([cos_t, sin_t]).astype(np.float32)
    span = np.stack([cos_s, sin_s])[:, :, None, :].astype(np.float32)
    return jnp.asarray(token), jnp.asarray(span)


def kernel(
    so_ref, q_in, k_in, v_in, do_in, qg_in, kg_in, tab_in, span_in,
    dq_hbm, dk_hbm, dv_hbm, dqg_hbm, dkg_hbm,
    qg_ref, kg_ref, tab_ref, span_ref, dq_out, dk_out, dv_out, dqg_out, dkg_out,
    sel_ref, low_ref, q_ref, k_ref, v_ref, do_ref,
    kv, kr, qs, qt, dos, dot_, rope, qi, ki,
    e_a, e_b, dp_a, dp_b, mh, lh, dh, ml, ll, dl, fh, fl, delta,
    pb, dsb, acc, cb, stage, gotr, pstage, gotp, sg, dkn,
    stat, inv_buf, gain_buf,
    in_sem, out_sem, relay, ag_ssem, ag_rsem, rs_ssem, rs_rsem, ps_ssem, ps_rsem,
    st_ssem, st_rsem, iv_ssem, iv_rsem, gn_ssem, gn_rsem,
):
    loads = [
        pltpu.make_async_copy(source, target, in_sem.at[number])
        for number, (source, target) in enumerate(
            (
                (k_in, k_ref), (v_in, v_ref), (q_in, q_ref), (do_in, do_ref),
                (qg_in, qg_ref), (kg_in, kg_ref), (tab_in, tab_ref), (span_in, span_ref),
            )
        )
    ]
    for load in loads:
        load.start()

    ctx = lax.axis_index("ctx")
    tp = lax.axis_index("tp")
    z, x = ctx // RING, ctx % RING
    flip = tp % 2
    turned_z = [z] + [(z + jnp.where(flip == 0, o, RING - o)) % RING for o in (1, 2, 3)]
    turned_x = [x] + [(x + jnp.where(flip == 0, o, RING - o)) % RING for o in (1, 2, 3)]
    peers = {(oz, ox): turned_z[oz] * RING + turned_x[ox] for oz, ox in ORDER}
    tp_peers = [(tp + offset) % 8 for offset in range(8)]

    def to_ctx(pair):
        return {"ctx": peers[pair]}

    barrier = pltpu.get_barrier_semaphore()
    for pair in RINGS:
        pl.semaphore_signal(
            barrier, inc=1, device_id=to_ctx(pair), device_id_type=pl.DeviceIdType.MESH
        )
    for offset in range(1, 8):
        pl.semaphore_signal(
            barrier, inc=1, device_id={"tp": tp_peers[offset]},
            device_id_type=pl.DeviceIdType.MESH,
        )

    s0, s1 = so_ref[2 * ctx], so_ref[2 * ctx + 1]
    low = jnp.minimum(s0, s1)
    offs = (jnp.where(s0 < s1, 0, 1), jnp.where(s0 < s1, 1, 0))
    low_ref[0] = low
    for slot in range(1, SLOTS):
        other = peers[ORDER[slot]]
        a = jnp.minimum(so_ref[2 * other], so_ref[2 * other + 1])
        low_ref[slot] = a
        sel_ref[slot] = jnp.where(a < low, 1, 0)

    loads[0].wait()
    loads[1].wait()
    for half in (LOW, HIGH):
        kv[half, 0, KEY] = k_ref[offs[half]]
        kv[half, 0, VAL] = v_ref[offs[half]]

    pl.semaphore_wait(barrier, 13)

    axis_of = {LOW: ("x", "z"), HIGH: ("z", "x")}

    def neighbour(half, axis, step):
        return to_ctx((step, 0) if axis_of[half][axis] == "z" else (0, step))

    def gather_copy(half, slot, axis, step, dst):
        return pltpu.make_async_remote_copy(
            src_ref=kv.at[half, slot],
            dst_ref=kv.at[half, dst],
            send_sem=ag_ssem.at[half, dst],
            recv_sem=ag_rsem.at[half, dst],
            device_id=neighbour(half, axis, step),
            device_id_type=pl.DeviceIdType.MESH,
        )

    def gather_forward(half, slot):
        for axis, step, dst in gather_sends(half, slot):
            gather_copy(half, slot, axis, step, dst).start()

    def hop(slots):
        for slot in slots:
            for half in (LOW, HIGH):
                gather_copy(half, slot, 0, 1, slot).wait_recv()
                gather_forward(half, slot)

    gather_forward(LOW, 0)
    gather_forward(HIGH, 0)
    for pair in RINGS[3:]:
        pl.semaphore_signal(
            relay, inc=1, device_id=to_ctx(pair), device_id_type=pl.DeviceIdType.MESH
        )

    def stat_copy(kind, offset):
        return pltpu.make_async_remote_copy(
            src_ref=stat.at[kind, 0],
            dst_ref=stat.at[kind, offset],
            send_sem=st_ssem.at[kind, offset],
            recv_sem=st_rsem.at[kind, offset],
            device_id={"tp": tp_peers[offset]},
            device_id_type=pl.DeviceIdType.MESH,
        )

    def stat_send(kind):
        for offset in range(1, 8):
            stat_copy(kind, offset).start()

    def stat_total(kind):
        total = stat[kind, 0]
        for offset in range(1, 8):
            stat_copy(kind, offset).wait_recv()
            total = total + stat[kind, offset]
        return total

    def token_sums(square):
        return jnp.sum(jnp.transpose(square), axis=0, keepdims=True)

    def spread(row):
        return jnp.transpose(jnp.broadcast_to(row, (SPAN, SPAN)))

    def head(number):
        return slice(number * DH, (number + 1) * DH)

    def q_gain_row(h):
        return qg_ref[head(h)].reshape(1, DH)

    def k_gain_row():
        return kg_ref[...].reshape(1, DH)

    for load in loads[2:]:
        load.wait()
    stat[0, 0] = jnp.zeros((8, SPAN), F32)
    for half in (LOW, HIGH):
        square = jnp.zeros((SPAN, DH), F32)
        for h in range(GROUP):
            part = q_ref[offs[half], :, head(h)].astype(F32)
            square = square + part * part
        stat[0, 0, half:half + 1, :] = token_sums(square)
        part = kv[half, 0, KEY].astype(F32)
        stat[0, 0, 2 + half:3 + half, :] = token_sums(part * part)
    stat_send(0)

    def rope_tables(span):
        cos_t, sin_t = tab_ref[0], tab_ref[1]
        cos_s, sin_s = span_ref[0, span], span_ref[1, span]
        return cos_s * cos_t - sin_s * sin_t, sin_s * cos_t + cos_s * sin_t

    for half, span in ((LOW, low), (HIGH, SPANS - 1 - low)):
        rope[half, 0], rope[half, 1] = rope_tables(span)
    for half in (LOW, HIGH):
        for h in range(GROUP):
            part = do_ref[offs[half], :, head(h)]
            dos[half, head(h), :] = part
            dot_[half, :, head(h)] = jnp.transpose(part)

    def rotated(half, part, sign):
        turned = pltpu.roll(part, DH // 2, 1) * rope[half, 1]
        straight = part * rope[half, 0]
        return straight + turned if sign > 0 else straight - turned

    total = stat_total(0)
    pl.semaphore_wait(relay, 3)
    inv_buf[0] = lax.rsqrt(total / KVD + EPS)
    q_inv = lax.rsqrt(total / D + EPS)

    def inv_copy(slot):
        return pltpu.make_async_remote_copy(
            src_ref=inv_buf.at[0],
            dst_ref=inv_buf.at[MIRROR[slot]],
            send_sem=iv_ssem.at[slot],
            recv_sem=iv_rsem.at[MIRROR[slot]],
            device_id=to_ctx(ORDER[slot]),
            device_id_type=pl.DeviceIdType.MESH,
        )

    for slot in range(1, SLOTS):
        inv_copy(slot).start()

    hop((1, 2, 3, 4))

    for half in (LOW, HIGH):
        ki[half] = spread(inv_buf[0, 2 + half:3 + half, :])
        part = kv[half, 0, KEY].astype(F32) * ki[half] * k_gain_row()
        kr[half, 0] = rotated(half, part, 1).astype(BF16)
        qi[half] = spread(q_inv[half:half + 1, :])
        for h in range(GROUP):
            part = q_ref[offs[half], :, head(h)].astype(F32) * qi[half] * q_gain_row(h)
            turned = rotated(half, part, 1).astype(BF16)
            qs[half, head(h), :] = turned
            qt[half, :, head(h)] = jnp.transpose(turned)

    hop((5, 6))

    def mm(a, b):
        return jnp.dot(a, b, preferred_element_type=F32)

    def pick(is_low, low_rows, high_rows):
        return jnp.where(is_low, low_rows, high_rows)

    def key_rows(half, slot):
        span = low_ref[slot] if half == LOW else SPANS - 1 - low_ref[slot]
        cos, sin = rope_tables(span)
        part = kv[half, slot, KEY].astype(F32)
        part = part * spread(inv_buf[slot, 2 + half:3 + half, :]) * k_gain_row()
        part = part * cos + pltpu.roll(part, DH // 2, 1) * sin
        kr[half, slot] = part.astype(BF16)

    def values_pass(slot):
        is_low = sel_ref[slot] == 1
        other = 1 - sel_ref[slot]
        v_low = kv[LOW, slot, VAL]
        v_other = pick(is_low, v_low, kv[HIGH, slot, VAL])
        for start, width in CHUNKS:
            cols = pl.ds(start, width)
            dp_a[slot, :, cols] = mm(v_low, dot_[HIGH, :, cols])
            dp_b[slot, :, cols] = mm(v_other, dot_[other, :, cols])

    def scores(keys, half, cols, d_probs, exps, slot, mask=None):
        s = mm(keys, qt[half, :, cols])
        if mask is not None:
            s = jnp.where(mask, s, NEG)
        top = jnp.max(s, axis=0, keepdims=True)
        e = jnp.exp2(s * C2 - top * C2)
        exps[slot, :, cols] = e
        return (
            top,
            jnp.sum(e, axis=0, keepdims=True),
            jnp.sum(e * d_probs[slot, :, cols], axis=0, keepdims=True),
        )

    def put(tabs, row, cols, stats):
        for tab, value in zip(tabs, stats):
            tab[row, :, cols] = value

    tabs_high, tabs_low = (mh, lh, dh), (ml, ll, dl)

    def keys_pass(slot):
        chosen = sel_ref[slot]
        is_low = chosen == 1
        for half in (LOW, HIGH):
            key_rows(half, slot)
        k_low = kr[LOW, slot]
        k_other = pick(is_low, k_low, kr[HIGH, slot])
        for start, width in CHUNKS:
            cols = pl.ds(start, width)
            put(tabs_high, slot, cols, scores(k_low, HIGH, cols, dp_a, e_a, slot))
            top, total, dots = scores(k_other, 1 - chosen, cols, dp_b, e_b, slot)
            put(tabs_high, slot + 15, cols, (jnp.where(is_low, NEG, top), total, dots))
            put(tabs_low, slot, cols, (jnp.where(is_low, top, NEG), total, dots))

    def own_values():
        for start, width in CHUNKS:
            cols = pl.ds(start, width)
            dp_a[0, :, cols] = mm(kv[LOW, 0, VAL], dot_[HIGH, :, cols])
            dp_b[0, :, cols] = mm(kv[LOW, 0, VAL], dot_[LOW, :, cols])
            dp_b[16, :, cols] = mm(kv[HIGH, 0, VAL], dot_[HIGH, :, cols])

    def own_keys():
        for start, width in CHUNKS:
            cols = pl.ds(start, width)
            shape = (SPAN, width)
            mask = lax.broadcasted_iota(jnp.int32, shape, 0) <= (
                lax.broadcasted_iota(jnp.int32, shape, 1) % SPAN
            )
            put(tabs_high, 0, cols, scores(kr[LOW, 0], HIGH, cols, dp_a, e_a, 0))
            put(tabs_low, 0, cols, scores(kr[LOW, 0], LOW, cols, dp_b, e_b, 0, mask))
            put(tabs_high, 31, cols, scores(kr[HIGH, 0], HIGH, cols, dp_b, e_b, 16, mask))

    def over(first, last, step):
        lax.fori_loop(first, last, lambda slot, _: (step(slot), 0)[1], 0)

    own_values()
    own_keys()
    over(1, 5, values_pass)
    hop((7, 8, 9))
    over(5, 7, values_pass)
    for slot in range(1, SLOTS):
        inv_copy(MIRROR[slot]).wait_recv()
    over(1, 7, keys_pass)
    hop((10, 11, 12))
    over(7, 13, values_pass)
    over(7, 10, keys_pass)
    hop((13, 14, 15))
    over(10, 13, keys_pass)
    over(13, 16, values_pass)
    over(13, 16, keys_pass)

    def finish(tabs, factors, half):
        tops, sums, dots = (tab[...] for tab in tabs)
        weights = jnp.exp2((tops - jnp.max(tops, axis=0, keepdims=True)) * C2)
        scale = 1.0 / jnp.sum(weights * sums, axis=0, keepdims=True)
        delta[half] = (jnp.sum(weights * dots, axis=0, keepdims=True) * scale)[0]
        factors[...] = weights * scale

    finish(tabs_high, fh, HIGH)
    finish(tabs_low, fl, LOW)

    def grads(exps, d_probs, slot, factor, shift, where):
        for start, width in CHUNKS:
            cols = pl.ds(start, width)
            probs = exps[slot, :, cols] * factor(cols)
            d_scores = probs * (d_probs[slot, :, cols] - shift(cols))
            pb[where, :, cols] = probs.astype(BF16)
            dsb[pl.ds(where * SPAN, SPAN), cols] = d_scores.astype(BF16)

    def rows(where):
        return pl.ds(where * SPAN, SPAN)

    def second_pass(slot):
        chosen = sel_ref[slot]
        is_low = chosen == 1
        other = 1 - chosen
        grads(e_a, dp_a, slot, lambda c: fh[slot, :, c], lambda c: delta[HIGH, :, c], 0)
        grads(
            e_b, dp_b, slot,
            lambda c: fl[slot, :, c] + fh[slot + 15, :, c],
            lambda c: delta[other, :, c], 1,
        )
        for kind, left in ((0, None), (1, None)):
            a_rows = pb[0] if kind == 0 else dsb[rows(0), :]
            b_rows = pb[1] if kind == 0 else dsb[rows(1), :]
            source = dos if kind == 0 else qs
            from_a = mm(a_rows, source[HIGH])
            from_b = mm(b_rows, source[other])
            cb[slot, LOW, kind] = from_a + jnp.where(is_low, from_b, 0.0)
            cb[slot, HIGH, kind] = jnp.where(is_low, 0.0, from_b)
        turned_low = jnp.transpose(kr[LOW, slot])
        turned_other = jnp.transpose(pick(is_low, kr[LOW, slot], kr[HIGH, slot]))
        none = jnp.zeros_like(turned_other)
        both = jnp.concatenate([turned_low, jnp.where(is_low, none, turned_other)], axis=1)
        only_low = jnp.where(is_low, turned_other, none)
        for start, width in CHUNKS:
            cols = pl.ds(start, width)
            acc[HIGH, :, cols] += mm(both, dsb[0:2 * SPAN, cols])
            acc[LOW, :, cols] += mm(only_low, dsb[rows(1), cols])

    def own_second():
        grads(e_a, dp_a, 0, lambda c: fh[0, :, c], lambda c: delta[HIGH, :, c], 0)
        grads(e_b, dp_b, 16, lambda c: fh[31, :, c], lambda c: delta[HIGH, :, c], 1)
        grads(e_b, dp_b, 0, lambda c: fl[0, :, c], lambda c: delta[LOW, :, c], 2)
        for kind in (0, 1):
            source = dos if kind == 0 else qs
            parts = [pb[i] if kind == 0 else dsb[rows(i), :] for i in range(3)]
            cb[0, LOW, kind] = mm(parts[0], source[HIGH]) + mm(parts[2], source[LOW])
            cb[0, HIGH, kind] = mm(parts[1], source[HIGH])
        turned_low = jnp.transpose(kr[LOW, 0])
        turned_high = jnp.transpose(kr[HIGH, 0])
        both = jnp.concatenate([turned_low, turned_high], axis=1)
        for start, width in CHUNKS:
            cols = pl.ds(start, width)
            acc[HIGH, :, cols] += mm(both, dsb[0:2 * SPAN, cols])
            acc[LOW, :, cols] += mm(turned_low, dsb[rows(2), cols])

    acc[...] = jnp.zeros_like(acc)

    def ring_copy(half, first, second):
        return pltpu.make_async_remote_copy(
            src_ref=stage.at[half, first, second],
            dst_ref=gotr.at[half, first, second],
            send_sem=rs_ssem.at[half, first, second],
            recv_sem=rs_rsem.at[half, first, second],
            device_id=neighbour(half, 1, second),
            device_id_type=pl.DeviceIdType.MESH,
        )

    def last_copy(half, first):
        return pltpu.make_async_remote_copy(
            src_ref=pstage.at[half, first],
            dst_ref=gotp.at[half, first],
            send_sem=ps_ssem.at[half, first],
            recv_sem=ps_rsem.at[half, first],
            device_id=neighbour(half, 0, first),
            device_id_type=pl.DeviceIdType.MESH,
        )

    def ring_send(half, slot):
        first, second = primary_view(half, slot)
        if second:
            stage[half, first, second] = cb[slot, half].astype(BF16)
            ring_copy(half, first, second).start()

    def ring_sum(half, first):
        total = cb[slot_of(half, first, 0), half]
        for second in (1, 2, 3):
            ring_copy(half, first, second).wait_recv()
            total = total + gotr[half, first, second].astype(F32)
        return total

    def last_send(first):
        for half in (LOW, HIGH):
            pstage[half, first] = ring_sum(half, first).astype(BF16)
            last_copy(half, first).start()

    def last_sum(half):
        total = ring_sum(half, 0)
        for first in (2, 1, 3):
            last_copy(half, first).wait_recv()
            total = total + gotp[half, first].astype(F32)
        return total

    def run_events(slot):
        for half in (LOW, HIGH):
            ring_send(half, slot)
        if slot == 2:
            last_send(2)

    def second_step(number, carry):
        slot = SLOTS - 1 - number
        second_pass(slot)
        for which in range(1, SLOTS):
            pl.when(slot == which)(functools.partial(run_events, which))
        return carry

    lax.fori_loop(0, SLOTS - 1, second_step, 0)
    own_second()
    stat[1, 0] = jnp.zeros((8, SPAN), F32)
    gain_buf[0] = jnp.zeros((8, DH), F32)
    for half in (LOW, HIGH):
        inner = jnp.zeros((SPAN, DH), F32)
        for h in range(GROUP):
            d_rot = jnp.transpose(acc[half, :, head(h)]) * SCALE
            d_norm = rotated(half, d_rot, -1)
            q_hat = q_ref[offs[half], :, head(h)].astype(F32) * qi[half]
            gain_buf[0, h:h + 1, :] += jnp.sum(d_norm * q_hat, axis=0, keepdims=True)
            scaled = d_norm * q_gain_row(h)
            sg[half, :, head(h)] = scaled
            inner = inner + scaled * q_hat
        stat[1, 0, half:half + 1, :] = token_sums(inner)
    stat_send(1)

    last_send(1)
    last_send(3)

    q_inner = stat_total(1) / D
    for half in (LOW, HIGH):
        inner = spread(q_inner[half:half + 1, :])
        for h in range(GROUP):
            q_hat = q_ref[offs[half], :, head(h)].astype(F32) * qi[half]
            sg[half, :, head(h)] = qi[half] * (sg[half, :, head(h)] - q_hat * inner)

    first_half = jnp.where(s0 < s1, LOW, HIGH)
    places = ((0, first_half), (1, 1 - first_half))
    for place, half in places:
        dq_out[place * SPAN:(place + 1) * SPAN, :] = sg[half].astype(BF16)

    def store(number, source, target):
        return pltpu.make_async_copy(source, target, out_sem.at[number])

    stores = [
        store(number, source, target)
        for number, (source, target) in enumerate(
            (
                (dq_out, dq_hbm), (dk_out, dk_hbm), (dv_out, dv_hbm),
                (dqg_out, dqg_hbm), (dkg_out, dkg_hbm),
            )
        )
    ]
    stores[0].start()

    stat[2, 0] = jnp.zeros((8, SPAN), F32)
    for half in (LOW, HIGH):
        summed = last_sum(half)
        dkn[1, half] = summed[0]
        d_norm = rotated(half, summed[1] * SCALE, -1)
        k_hat = kv[half, 0, KEY].astype(F32) * ki[half]
        gain_buf[0, 5:6, :] += jnp.sum(d_norm * k_hat, axis=0, keepdims=True)
        scaled = d_norm * k_gain_row()
        dkn[0, half] = scaled
        stat[2, 0, half:half + 1, :] = token_sums(scaled * k_hat)

    def gain_copy(slot):
        return pltpu.make_async_remote_copy(
            src_ref=gain_buf.at[0],
            dst_ref=gain_buf.at[slot],
            send_sem=gn_ssem.at[slot],
            recv_sem=gn_rsem.at[slot],
            device_id=to_ctx(ORDER[slot]),
            device_id_type=pl.DeviceIdType.MESH,
        )

    for slot in range(SLOTS - 1, 0, -1):
        gain_copy(slot).start()
    stat_send(2)

    for place, half in places:
        dv_out[place * SPAN:(place + 1) * SPAN, :] = dkn[1, half].astype(BF16)
    stores[2].start()

    k_inner = stat_total(2) / KVD
    for half in (LOW, HIGH):
        inner = spread(k_inner[half:half + 1, :])
        k_hat = kv[half, 0, KEY].astype(F32) * ki[half]
        dkn[0, half] = ki[half] * (dkn[0, half] - k_hat * inner)
    for place, half in places:
        dk_out[place * SPAN:(place + 1) * SPAN, :] = dkn[0, half].astype(BF16)
    stores[1].start()

    total = gain_buf[0]
    for slot in range(1, SLOTS):
        gain_copy(slot).wait_recv()
        total = total + gain_buf[slot]
    for h in range(GROUP):
        dqg_out[head(h)] = total[h:h + 1, :].reshape(DH)
    dkg_out[...] = total[5:6, :].reshape(DH)
    stores[3].start()
    stores[4].start()

    for item in stores:
        item.wait()
    for half in (LOW, HIGH):
        for slot in range(SLOTS):
            for axis, step, dst in gather_sends(half, slot):
                gather_copy(half, slot, axis, step, dst).wait_send()
            first, second = primary_view(half, slot)
            if second:
                ring_copy(half, first, second).wait_send()
        for first in (1, 2, 3):
            last_copy(half, first).wait_send()
    for kind in range(3):
        for offset in range(1, 8):
            stat_copy(kind, offset).wait_send()
    for slot in range(1, SLOTS):
        inv_copy(slot).wait_send()
        gain_copy(slot).wait_send()


def pass_on(*refs):
    for source, target in zip(refs[:5], refs[5:]):
        target[...] = source[...]


def per_device(q_raw, k_raw, values, d_out, q_gain, k_gain, span_order):
    token_table, span_table = tables()
    smem = pl.BlockSpec(memory_space=pltpu.SMEM)
    tile = (SPAN, DH)
    dma = pltpu.SemaphoreType.DMA
    wide = (SPAN, QW)
    scratch = [
        pltpu.VMEM((QW,), F32), pltpu.VMEM((DH,), F32),
        pltpu.VMEM((2,) + tile, F32), pltpu.VMEM((2, SPANS, 1, DH), F32),
        pltpu.VMEM((2 * SPAN, QW), BF16), pltpu.VMEM((2 * SPAN, DH), BF16),
        pltpu.VMEM((2 * SPAN, DH), BF16), pltpu.VMEM((QW,), F32), pltpu.VMEM((DH,), F32),
        pltpu.SMEM((SLOTS,), jnp.int32),
        pltpu.SMEM((SLOTS,), jnp.int32),
        pltpu.VMEM((2,) + wide, BF16),
        pltpu.VMEM((2,) + tile, BF16),
        pltpu.VMEM((2,) + tile, BF16),
        pltpu.VMEM((2,) + wide, BF16),
        pltpu.VMEM((2, SLOTS, 2) + tile, BF16),
        pltpu.VMEM((2, SLOTS) + tile, BF16),
        pltpu.VMEM((2, QW, DH), BF16),
        pltpu.VMEM((2, DH, QW), BF16),
        pltpu.VMEM((2, QW, DH), BF16),
        pltpu.VMEM((2, DH, QW), BF16),
        pltpu.VMEM((2, 2) + tile, F32),
        pltpu.VMEM((2,) + tile, F32),
        pltpu.VMEM((2,) + tile, F32),
        pltpu.VMEM((16,) + wide, F32),
        pltpu.VMEM((17,) + wide, F32),
        pltpu.VMEM((16,) + wide, F32),
        pltpu.VMEM((17,) + wide, F32),
        pltpu.VMEM((32, 1, QW), F32),
        pltpu.VMEM((32, 1, QW), F32),
        pltpu.VMEM((32, 1, QW), F32),
        pltpu.VMEM((16, 1, QW), F32),
        pltpu.VMEM((16, 1, QW), F32),
        pltpu.VMEM((16, 1, QW), F32),
        pltpu.VMEM((32, 1, QW), F32),
        pltpu.VMEM((16, 1, QW), F32),
        pltpu.VMEM((2, 1, QW), F32),
        pltpu.VMEM((3,) + wide, BF16),
        pltpu.VMEM((3 * SPAN, QW), BF16),
        pltpu.VMEM((2,) + wide, F32),
        pltpu.VMEM((SLOTS, 2, 2) + tile, F32),
        pltpu.VMEM((2, RING, RING, 2) + tile, BF16),
        pltpu.VMEM((2, RING, RING, 2) + tile, BF16),
        pltpu.VMEM((2, RING, 2) + tile, BF16),
        pltpu.VMEM((2, RING, 2) + tile, BF16),
        pltpu.VMEM((2,) + wide, F32),
        pltpu.VMEM((2, 2) + tile, F32),
        pltpu.VMEM((3, 8, 8, SPAN), F32),
        pltpu.VMEM((SLOTS, 8, SPAN), F32),
        pltpu.VMEM((SLOTS, 8, DH), F32),
        dma((8,)), dma((5,)), pltpu.SemaphoreType.REGULAR,
        dma((2, SLOTS)), dma((2, SLOTS)),
        dma((2, RING, RING)), dma((2, RING, RING)),
        dma((2, RING)), dma((2, RING)),
        dma((3, 8)), dma((3, 8)),
        dma((SLOTS,)), dma((SLOTS,)),
        dma((SLOTS,)), dma((SLOTS,)),
    ]
    rows = 2 * SPAN
    shapes = (
        jax.ShapeDtypeStruct((rows, QW), BF16),
        jax.ShapeDtypeStruct((rows, DH), BF16),
        jax.ShapeDtypeStruct((rows, DH), BF16),
        jax.ShapeDtypeStruct((QW,), F32),
        jax.ShapeDtypeStruct((DH,), F32),
    )
    vmem = pl.BlockSpec(memory_space=pltpu.VMEM)
    hbm = pl.BlockSpec(memory_space=pltpu.HBM)
    results = pl.pallas_call(
        kernel,
        out_shape=shapes,
        in_specs=[smem] + [hbm] * 8,
        out_specs=(hbm,) * 5,
        scratch_shapes=scratch,
        compiler_params=pltpu.CompilerParams(
            collective_id=0, has_side_effects=True, vmem_limit_bytes=60 * 2**20
        ),
    )(
        span_order,
        q_raw.reshape(2, SPAN, QW), k_raw.reshape(2, SPAN, DH),
        values.reshape(2, SPAN, DH), d_out.reshape(2, SPAN, QW),
        q_gain, k_gain, token_table, span_table,
    )
    return pl.pallas_call(
        pass_on, out_shape=shapes, in_specs=[vmem] * 5, out_specs=(vmem,) * 5,
        compiler_params=pltpu.CompilerParams(vmem_limit_bytes=60 * 2**20),
    )(*results)


def solution(mesh):
    return jax.shard_map(
        per_device,
        mesh=mesh,
        in_specs=(
            P("ctx", "tp"),
            P("ctx", "tp"),
            P("ctx", "tp"),
            P("ctx", "tp"),
            P("tp"),
            P("tp"),
            P(),
        ),
        out_specs=(P("ctx", "tp"), P("ctx", "tp"), P("ctx", "tp"), P("tp"), P("tp")),
        check_vma=False,
    )
```

time: 71.3 us -> 59.2 us (0.83)
  the two profiles are of different devices: /device:TPU:1 before, /device:TPU:0 now
where the time goes in v2:
time: 59.2 us; the launch traced here: 59 us
  Pallas kernels  58.4 us (99%)
  between operations  0.64 us (1%)
    pallas_call x1, Pallas kernels, per_device(): pl.pallas_call(kernel, out_shape=shapes, in_specs=[smem] + [hbm] * 8, out...  56.6 us
    pallas_call x1, Pallas kernels, per_device(): pl.pallas_call(pass_on, out_shape=shapes, in_specs=[vmem] * 5, out_specs=...  1.79 us

profile of v2, /device:TPU:0, one launch (start us, length us, event | category | flops | bytes accessed | tf_op | source)
XLA Modules:
  0.0 59.0 jit_solution(13201004138630430002)
XLA Ops:
  0.6 56.6 %shard_map.128 = (bf16[256,640]{1,0:T(8,128)(2,1)}, bf16[256,128]{1,0:T(8,128)(2,1)}, bf16[256,128]{1,0:T(8,128)(2,1)}, f32[640]{0:T(1024)}, f32[128]{0:T(128)}) custom-call(s32[32]{0:T(128)} %so_ref.1, bf16[2,128,640]{2,1,0:T(8,128)(2,1)} %bitcast.4, bf16[2,128,128]{2,1,0:T(8,128)(2,1)} %bitcast.6, bf16[2,128,128]{2,1,0:T(8,128)(2,1)} %bitcast.7, ...), custom_call_target="tpu_custom_call" | custom-call | tf_op jit(solution)/shard_map/pallas_call | solution.py:689
  57.2 1.8 %shard_map.129 = (bf16[256,640]{1,0:T(8,128)(2,1)}, bf16[256,128]{1,0:T(8,128)(2,1)}, bf16[256,128]{1,0:T(8,128)(2,1)}, f32[640]{0:T(1024)}, f32[128]{0:T(128)}) custom-call(bf16[256,640]{1,0:T(8,128)(2,1)} %get-tuple-element.10.refs_0_, bf16[256,128]{1,0:T(8,128)(2,1)} %get-tuple-element.11.refs_1_, bf16[256,128]{1,0:T(8,128)(2,1)} %get-tuple-element.12.refs_2_, ...), custom_call_target="tpu_custom_call" | custom-call | tf_op jit(solution)/shard_map/pallas_call | solution.py:704

commit v3 on v2

--- a/solution.py
+++ b/solution.py
@@ -1,4 +1,3 @@
-import functools
 import math
 
 import jax
@@ -354,7 +353,8 @@
             put(tabs_high, 31, cols, scores(kr[HIGH, 0], HIGH, cols, dp_b, e_b, 16, mask))
 
     def over(first, last, step):
-        lax.fori_loop(first, last, lambda slot, _: (step(slot), 0)[1], 0)
+        for slot in range(first, last):
+            step(slot)
 
     own_values()
     own_keys()
@@ -446,7 +446,7 @@
             dst_ref=gotr.at[half, first, second],
             send_sem=rs_ssem.at[half, first, second],
             recv_sem=rs_rsem.at[half, first, second],
-            device_id=neighbour(half, 1, second),
+            device_id=neighbour(half, 1, 1 if first and second == 2 else second),
             device_id_type=pl.DeviceIdType.MESH,
         )
 
@@ -462,44 +462,51 @@
 
     def ring_send(half, slot):
         first, second = primary_view(half, slot)
-        if second:
+        if second > 1 or (second == 1 and first == 0):
             stage[half, first, second] = cb[slot, half].astype(BF16)
             ring_copy(half, first, second).start()
 
+    def near_send(first):
+        for half in (LOW, HIGH):
+            ring_copy(half, first, 2).wait_recv()
+            mixed = cb[slot_of(half, first, 1), half] + gotr[half, first, 2].astype(F32)
+            stage[half, first, 1] = mixed.astype(BF16)
+            ring_copy(half, first, 1).start()
+
     def ring_sum(half, first):
         total = cb[slot_of(half, first, 0), half]
-        for second in (1, 2, 3):
+        for second in (1, 3) if first else (1, 2, 3):
             ring_copy(half, first, second).wait_recv()
             total = total + gotr[half, first, second].astype(F32)
         return total
 
+    def gain_part(half, first, d_rot):
+        slot = slot_of(half, first, 0)
+        span = low_ref[slot] if half == LOW else SPANS - 1 - low_ref[slot]
+        cos, sin = rope_tables(span)
+        d_norm = d_rot * cos - pltpu.roll(d_rot, DH // 2, 1) * sin
+        k_hat = kv[half, slot, KEY].astype(F32) * spread(inv_buf[slot, 2 + half:3 + half, :])
+        gain_buf[0, 5:6, :] += jnp.sum(d_norm * k_hat, axis=0, keepdims=True)
+
     def last_send(first):
+        totals = []
         for half in (LOW, HIGH):
-            pstage[half, first] = ring_sum(half, first).astype(BF16)
+            totals.append(ring_sum(half, first))
+            pstage[half, first] = totals[half].astype(BF16)
             last_copy(half, first).start()
-
-    def last_sum(half):
-        total = ring_sum(half, 0)
-        for first in (2, 1, 3):
-            last_copy(half, first).wait_recv()
-            total = total + gotp[half, first].astype(F32)
-        return total
-
-    def run_events(slot):
+        for half in (LOW, HIGH):
+            gain_part(half, first, totals[half][1] * SCALE)
+
+    steps = (15, 14, 13, 12, 11, 7, 9, 8, 6, 5, 10, 4, 3, 2, 1)
+    near = {10: 2, 4: 1, 2: 3}
+    for slot in steps:
+        second_pass(slot)
         for half in (LOW, HIGH):
             ring_send(half, slot)
-        if slot == 2:
-            last_send(2)
-
-    def second_step(number, carry):
-        slot = SLOTS - 1 - number
-        second_pass(slot)
-        for which in range(1, SLOTS):
-            pl.when(slot == which)(functools.partial(run_events, which))
-        return carry
-
-    lax.fori_loop(0, SLOTS - 1, second_step, 0)
+        if slot in near:
+            near_send(near[slot])
     own_second()
+
     stat[1, 0] = jnp.zeros((8, SPAN), F32)
     gain_buf[0] = jnp.zeros((8, DH), F32)
     for half in (LOW, HIGH):
@@ -515,8 +522,8 @@
         stat[1, 0, half:half + 1, :] = token_sums(inner)
     stat_send(1)
 
-    last_send(1)
-    last_send(3)
+    for first in (2, 1, 3):
+        last_send(first)
 
     q_inner = stat_total(1) / D
     for half in (LOW, HIGH):
@@ -544,16 +551,9 @@
     ]
     stores[0].start()
 
-    stat[2, 0] = jnp.zeros((8, SPAN), F32)
-    for half in (LOW, HIGH):
-        summed = last_sum(half)
-        dkn[1, half] = summed[0]
-        d_norm = rotated(half, summed[1] * SCALE, -1)
-        k_hat = kv[half, 0, KEY].astype(F32) * ki[half]
-        gain_buf[0, 5:6, :] += jnp.sum(d_norm * k_hat, axis=0, keepdims=True)
-        scaled = d_norm * k_gain_row()
-        dkn[0, half] = scaled
-        stat[2, 0, half:half + 1, :] = token_sums(scaled * k_hat)
+    totals = [ring_sum(half, 0) for half in (LOW, HIGH)]
+    for half in (LOW, HIGH):
+        gain_part(half, 0, totals[half][1] * SCALE)
 
     def gain_copy(slot):
         return pltpu.make_async_remote_copy(
@@ -567,6 +567,19 @@
 
     for slot in range(SLOTS - 1, 0, -1):
         gain_copy(slot).start()
+
+    stat[2, 0] = jnp.zeros((8, SPAN), F32)
+    for half in (LOW, HIGH):
+        total = totals[half]
+        for first in (2, 1, 3):
+            last_copy(half, first).wait_recv()
+            total = total + gotp[half, first].astype(F32)
+        dkn[1, half] = total[0]
+        d_norm = rotated(half, total[1] * SCALE, -1)
+        k_hat = kv[half, 0, KEY].astype(F32) * ki[half]
+        scaled = d_norm * k_gain_row()
+        dkn[0, half] = scaled
+        stat[2, 0, half:half + 1, :] = token_sums(scaled * k_hat)
     stat_send(2)
 
     for place, half in places:

time: 59.2 us -> 53.6 us (0.905)
  the two profiles are of different devices: /device:TPU:0 before, /device:TPU:1 now
where the time goes in v3:
time: 53.6 us; the launch traced here: 53.4 us
  Pallas kernels  52.8 us (99%)
  between operations  0.64 us (1%)
    pallas_call x1, Pallas kernels, per_device(): pl.pallas_call(kernel, out_shape=shapes, in_specs=[smem] + [hbm] * 8, out...  51 us
    pallas_call x1, Pallas kernels, per_device(): pl.pallas_call(pass_on, out_shape=shapes, in_specs=[vmem] * 5, out_specs=...  1.79 us

profile of v3, /device:TPU:1, one launch (start us, length us, event | category | flops | bytes accessed | tf_op | source)
XLA Modules:
  0.0 53.4 jit_solution(10385188105669828642)
XLA Ops:
  0.6 51.0 %shard_map.128 = (bf16[256,640]{1,0:T(8,128)(2,1)}, bf16[256,128]{1,0:T(8,128)(2,1)}, bf16[256,128]{1,0:T(8,128)(2,1)}, f32[640]{0:T(1024)}, f32[128]{0:T(128)}) custom-call(s32[32]{0:T(128)} %so_ref.1, bf16[2,128,640]{2,1,0:T(8,128)(2,1)} %bitcast.4, bf16[2,128,128]{2,1,0:T(8,128)(2,1)} %bitcast.6, bf16[2,128,128]{2,1,0:T(8,128)(2,1)} %bitcast.7, ...), custom_call_target="tpu_custom_call" | custom-call | tf_op jit(solution)/shard_map/pallas_call | solution.py:702
  51.6 1.8 %shard_map.129 = (bf16[256,640]{1,0:T(8,128)(2,1)}, bf16[256,128]{1,0:T(8,128)(2,1)}, bf16[256,128]{1,0:T(8,128)(2,1)}, f32[640]{0:T(1024)}, f32[128]{0:T(128)}) custom-call(bf16[256,640]{1,0:T(8,128)(2,1)} %get-tuple-element.10.refs_0_, bf16[256,128]{1,0:T(8,128)(2,1)} %get-tuple-element.11.refs_1_, bf16[256,128]{1,0:T(8,128)(2,1)} %get-tuple-element.12.refs_2_, ...), custom_call_target="tpu_custom_call" | custom-call | tf_op jit(solution)/shard_map/pallas_call | solution.py:717

commit v4 on v3

--- a/solution.py
+++ b/solution.py
@@ -81,17 +81,18 @@
 
 
 def kernel(
-    so_ref, q_in, k_in, v_in, do_in, qg_in, kg_in, tab_in, span_in,
+    so_in, q_in, k_in, v_in, do_in, qg_in, kg_in, tab_in, span_in,
     dq_hbm, dk_hbm, dv_hbm, dqg_hbm, dkg_hbm,
-    qg_ref, kg_ref, tab_ref, span_ref, dq_out, dk_out, dv_out, dqg_out, dkg_out,
+    so_ref, qg_ref, kg_ref, tab_ref, span_ref, dq_out, dk_out, dv_out, dqg_out, dkg_out,
     sel_ref, low_ref, q_ref, k_ref, v_ref, do_ref,
     kv, kr, qs, qt, dos, dot_, rope, qi, ki,
     e_a, e_b, dp_a, dp_b, mh, lh, dh, ml, ll, dl, fh, fl, delta,
     pb, dsb, acc, cb, stage, gotr, pstage, gotp, sg, dkn,
     stat, inv_buf, gain_buf,
-    in_sem, out_sem, relay, ag_ssem, ag_rsem, rs_ssem, rs_rsem, ps_ssem, ps_rsem,
-    st_ssem, st_rsem, iv_ssem, iv_rsem, gn_ssem, gn_rsem,
+    in_sem, out_sem, relay, sent, ag_sem, rest_sem, far_sem, rs_sem, ps_sem, st_sem, small_sem,
 ):
+    order_load = pltpu.make_async_copy(so_in, so_ref, in_sem.at[8])
+    order_load.start()
     loads = [
         pltpu.make_async_copy(source, target, in_sem.at[number])
         for number, (source, target) in enumerate(
@@ -127,6 +128,7 @@
             device_id_type=pl.DeviceIdType.MESH,
         )
 
+    order_load.wait()
     s0, s1 = so_ref[2 * ctx], so_ref[2 * ctx + 1]
     low = jnp.minimum(s0, s1)
     offs = (jnp.where(s0 < s1, 0, 1), jnp.where(s0 < s1, 1, 0))
@@ -150,12 +152,17 @@
     def neighbour(half, axis, step):
         return to_ctx((step, 0) if axis_of[half][axis] == "z" else (0, step))
 
+    def gather_arrival(half, dst):
+        if dst < 10:
+            return ag_sem.at[half, dst]
+        return rest_sem.at[0 if dst < 13 else 1]
+
     def gather_copy(half, slot, axis, step, dst):
         return pltpu.make_async_remote_copy(
             src_ref=kv.at[half, slot],
             dst_ref=kv.at[half, dst],
-            send_sem=ag_ssem.at[half, dst],
-            recv_sem=ag_rsem.at[half, dst],
+            send_sem=sent.at[0],
+            recv_sem=gather_arrival(half, dst),
             device_id=neighbour(half, axis, step),
             device_id_type=pl.DeviceIdType.MESH,
         )
@@ -170,6 +177,12 @@
                 gather_copy(half, slot, 0, 1, slot).wait_recv()
                 gather_forward(half, slot)
 
+    def finished(block, sem):
+        pltpu.make_async_copy(block, block, sem).wait()
+
+    def rest(first):
+        finished(kv.at[:, pl.ds(first, 3)], rest_sem.at[0 if first < 13 else 1])
+
     gather_forward(LOW, 0)
     gather_forward(HIGH, 0)
     for pair in RINGS[3:]:
@@ -181,8 +194,8 @@
         return pltpu.make_async_remote_copy(
             src_ref=stat.at[kind, 0],
             dst_ref=stat.at[kind, offset],
-            send_sem=st_ssem.at[kind, offset],
-            recv_sem=st_rsem.at[kind, offset],
+            send_sem=sent.at[3],
+            recv_sem=st_sem.at[kind],
             device_id={"tp": tp_peers[offset]},
             device_id_type=pl.DeviceIdType.MESH,
         )
@@ -192,9 +205,9 @@
             stat_copy(kind, offset).start()
 
     def stat_total(kind):
+        finished(stat.at[kind, pl.ds(1, 7)], st_sem.at[kind])
         total = stat[kind, 0]
         for offset in range(1, 8):
-            stat_copy(kind, offset).wait_recv()
             total = total + stat[kind, offset]
         return total
 
@@ -253,8 +266,8 @@
         return pltpu.make_async_remote_copy(
             src_ref=inv_buf.at[0],
             dst_ref=inv_buf.at[MIRROR[slot]],
-            send_sem=iv_ssem.at[slot],
-            recv_sem=iv_rsem.at[MIRROR[slot]],
+            send_sem=sent.at[4],
+            recv_sem=small_sem.at[0],
             device_id=to_ctx(ORDER[slot]),
             device_id_type=pl.DeviceIdType.MESH,
         )
@@ -352,25 +365,23 @@
             put(tabs_low, 0, cols, scores(kr[LOW, 0], LOW, cols, dp_b, e_b, 0, mask))
             put(tabs_high, 31, cols, scores(kr[HIGH, 0], HIGH, cols, dp_b, e_b, 16, mask))
 
-    def over(first, last, step):
-        for slot in range(first, last):
+    def each(step, slots):
+        for slot in slots:
             step(slot)
 
     own_values()
     own_keys()
-    over(1, 5, values_pass)
+    each(values_pass, (1, 2, 3, 4))
     hop((7, 8, 9))
-    over(5, 7, values_pass)
-    for slot in range(1, SLOTS):
-        inv_copy(MIRROR[slot]).wait_recv()
-    over(1, 7, keys_pass)
-    hop((10, 11, 12))
-    over(7, 13, values_pass)
-    over(7, 10, keys_pass)
-    hop((13, 14, 15))
-    over(10, 13, keys_pass)
-    over(13, 16, values_pass)
-    over(13, 16, keys_pass)
+    each(values_pass, (5, 6))
+    finished(inv_buf.at[pl.ds(1, SLOTS - 1)], small_sem.at[0])
+    each(keys_pass, (1, 2, 3, 4, 5, 6))
+    rest(10)
+    each(values_pass, (7, 8, 9, 10, 11, 12))
+    each(keys_pass, (7, 8, 9, 10, 11, 12))
+    rest(13)
+    each(values_pass, (13, 14, 15))
+    each(keys_pass, (13, 14, 15))
 
     def finish(tabs, factors, half):
         tops, sums, dots = (tab[...] for tab in tabs)
@@ -440,13 +451,16 @@
 
     acc[...] = jnp.zeros_like(acc)
 
-    def ring_copy(half, first, second):
+    PLACE = {1: 1, 3: 2, 2: 3}
+
+    def ring_copy(half, first, place):
+        step = {1: 1, 2: 3, 3: 1 if first else 2}[place]
         return pltpu.make_async_remote_copy(
-            src_ref=stage.at[half, first, second],
-            dst_ref=gotr.at[half, first, second],
-            send_sem=rs_ssem.at[half, first, second],
-            recv_sem=rs_rsem.at[half, first, second],
-            device_id=neighbour(half, 1, 1 if first and second == 2 else second),
+            src_ref=stage.at[half, first, place],
+            dst_ref=gotr.at[half, first, place],
+            send_sem=sent.at[1],
+            recv_sem=(far_sem if first and place == 3 else rs_sem).at[half, first],
+            device_id=neighbour(half, 1, step),
             device_id_type=pl.DeviceIdType.MESH,
         )
 
@@ -454,8 +468,8 @@
         return pltpu.make_async_remote_copy(
             src_ref=pstage.at[half, first],
             dst_ref=gotp.at[half, first],
-            send_sem=ps_ssem.at[half, first],
-            recv_sem=ps_rsem.at[half, first],
+            send_sem=sent.at[2],
+            recv_sem=ps_sem.at[half],
             device_id=neighbour(half, 0, first),
             device_id_type=pl.DeviceIdType.MESH,
         )
@@ -463,21 +477,22 @@
     def ring_send(half, slot):
         first, second = primary_view(half, slot)
         if second > 1 or (second == 1 and first == 0):
-            stage[half, first, second] = cb[slot, half].astype(BF16)
-            ring_copy(half, first, second).start()
+            stage[half, first, PLACE[second]] = cb[slot, half].astype(BF16)
+            ring_copy(half, first, PLACE[second]).start()
 
     def near_send(first):
         for half in (LOW, HIGH):
-            ring_copy(half, first, 2).wait_recv()
-            mixed = cb[slot_of(half, first, 1), half] + gotr[half, first, 2].astype(F32)
+            ring_copy(half, first, 3).wait_recv()
+            mixed = cb[slot_of(half, first, 1), half] + gotr[half, first, 3].astype(F32)
             stage[half, first, 1] = mixed.astype(BF16)
             ring_copy(half, first, 1).start()
 
     def ring_sum(half, first):
+        count = 2 if first else 3
+        finished(gotr.at[half, first, pl.ds(1, count)], rs_sem.at[half, first])
         total = cb[slot_of(half, first, 0), half]
-        for second in (1, 3) if first else (1, 2, 3):
-            ring_copy(half, first, second).wait_recv()
-            total = total + gotr[half, first, second].astype(F32)
+        for place in range(1, count + 1):
+            total = total + gotr[half, first, place].astype(F32)
         return total
 
     def gain_part(half, first, d_rot):
@@ -559,8 +574,8 @@
         return pltpu.make_async_remote_copy(
             src_ref=gain_buf.at[0],
             dst_ref=gain_buf.at[slot],
-            send_sem=gn_ssem.at[slot],
-            recv_sem=gn_rsem.at[slot],
+            send_sem=sent.at[5],
+            recv_sem=small_sem.at[1],
             device_id=to_ctx(ORDER[slot]),
             device_id_type=pl.DeviceIdType.MESH,
         )
@@ -570,9 +585,9 @@
 
     stat[2, 0] = jnp.zeros((8, SPAN), F32)
     for half in (LOW, HIGH):
+        finished(gotp.at[half, pl.ds(1, 3)], ps_sem.at[half])
         total = totals[half]
         for first in (2, 1, 3):
-            last_copy(half, first).wait_recv()
             total = total + gotp[half, first].astype(F32)
         dkn[1, half] = total[0]
         d_norm = rotated(half, total[1] * SCALE, -1)
@@ -595,9 +610,9 @@
         dk_out[place * SPAN:(place + 1) * SPAN, :] = dkn[0, half].astype(BF16)
     stores[1].start()
 
+    finished(gain_buf.at[pl.ds(1, SLOTS - 1)], small_sem.at[1])
     total = gain_buf[0]
     for slot in range(1, SLOTS):
-        gain_copy(slot).wait_recv()
         total = total + gain_buf[slot]
     for h in range(GROUP):
         dqg_out[head(h)] = total[h:h + 1, :].reshape(DH)
@@ -605,23 +620,14 @@
     stores[3].start()
     stores[4].start()
 
+    finished(kv.at[:, pl.ds(0, SLOTS - 1)], sent.at[0])
+    finished(stage.at[:, :, pl.ds(1, 3)], sent.at[1])
+    finished(pstage.at[:, pl.ds(1, 3)], sent.at[2])
+    finished(stat.at[:, pl.ds(1, 7)], sent.at[3])
+    finished(inv_buf.at[pl.ds(1, SLOTS - 1)], sent.at[4])
+    finished(gain_buf.at[pl.ds(1, SLOTS - 1)], sent.at[5])
     for item in stores:
         item.wait()
-    for half in (LOW, HIGH):
-        for slot in range(SLOTS):
-            for axis, step, dst in gather_sends(half, slot):
-                gather_copy(half, slot, axis, step, dst).wait_send()
-            first, second = primary_view(half, slot)
-            if second:
-                ring_copy(half, first, second).wait_send()
-        for first in (1, 2, 3):
-            last_copy(half, first).wait_send()
-    for kind in range(3):
-        for offset in range(1, 8):
-            stat_copy(kind, offset).wait_send()
-    for slot in range(1, SLOTS):
-        inv_copy(slot).wait_send()
-        gain_copy(slot).wait_send()
 
 
 def pass_on(*refs):
@@ -631,11 +637,11 @@
 
 def per_device(q_raw, k_raw, values, d_out, q_gain, k_gain, span_order):
     token_table, span_table = tables()
-    smem = pl.BlockSpec(memory_space=pltpu.SMEM)
     tile = (SPAN, DH)
     dma = pltpu.SemaphoreType.DMA
     wide = (SPAN, QW)
     scratch = [
+        pltpu.SMEM((SPANS,), jnp.int32),
         pltpu.VMEM((QW,), F32), pltpu.VMEM((DH,), F32),
         pltpu.VMEM((2,) + tile, F32), pltpu.VMEM((2, SPANS, 1, DH), F32),
         pltpu.VMEM((2 * SPAN, QW), BF16), pltpu.VMEM((2 * SPAN, DH), BF16),
@@ -681,13 +687,11 @@
         pltpu.VMEM((3, 8, 8, SPAN), F32),
         pltpu.VMEM((SLOTS, 8, SPAN), F32),
         pltpu.VMEM((SLOTS, 8, DH), F32),
-        dma((8,)), dma((5,)), pltpu.SemaphoreType.REGULAR,
-        dma((2, SLOTS)), dma((2, SLOTS)),
-        dma((2, RING, RING)), dma((2, RING, RING)),
+        dma((9,)), dma((5,)), pltpu.SemaphoreType.REGULAR,
+        dma((6,)),
+        dma((2, 10)), dma((2,)),
         dma((2, RING)), dma((2, RING)),
-        dma((3, 8)), dma((3, 8)),
-        dma((SLOTS,)), dma((SLOTS,)),
-        dma((SLOTS,)), dma((SLOTS,)),
+        dma((2,)), dma((3,)), dma((2,)),
     ]
     rows = 2 * SPAN
     shapes = (
@@ -702,7 +706,7 @@
     results = pl.pallas_call(
         kernel,
         out_shape=shapes,
-        in_specs=[smem] + [hbm] * 8,
+        in_specs=[hbm] * 9,
         out_specs=(hbm,) * 5,
         scratch_shapes=scratch,
         compiler_params=pltpu.CompilerParams(

time: 53.6 us -> 50.8 us (0.948)
  Pallas kernels: 52.8 us -> 50 us
    pallas_call x1, Pallas kernels: 51 us -> 48.2 us  [per_device(): pl.pallas_call(kernel, out_shape=shapes, in_specs=[hbm] * 9, out_specs=(h...]
where the time goes in v4:
time: 50.8 us; the launch traced here: 50.6 us
  Pallas kernels  50 us (98%)
  between operations  0.64 us (1%)
    pallas_call x1, Pallas kernels, per_device(): pl.pallas_call(kernel, out_shape=shapes, in_specs=[hbm] * 9, out_specs=(h...  48.2 us
    pallas_call x1, Pallas kernels, per_device(): pl.pallas_call(pass_on, out_shape=shapes, in_specs=[vmem] * 5, out_specs=...  1.79 us

profile of v4, /device:TPU:1, one launch (start us, length us, event | category | flops | bytes accessed | tf_op | source)
XLA Modules:
  0.0 50.6 jit_solution(3189606367999324712)
XLA Ops:
  0.6 48.2 %shard_map.128 = (bf16[256,640]{1,0:T(8,128)(2,1)}, bf16[256,128]{1,0:T(8,128)(2,1)}, bf16[256,128]{1,0:T(8,128)(2,1)}, f32[640]{0:T(1024)}, f32[128]{0:T(128)}) custom-call(s32[32]{0:T(128)} %so_in.1, bf16[2,128,640]{2,1,0:T(8,128)(2,1)} %bitcast.4, bf16[2,128,128]{2,1,0:T(8,128)(2,1)} %bitcast.6, bf16[2,128,128]{2,1,0:T(8,128)(2,1)} %bitcast.7, ...), custom_call_target="tpu_custom_call" | custom-call | tf_op jit(solution)/shard_map/pallas_call | solution.py:706
  48.8 1.8 %shard_map.129 = (bf16[256,640]{1,0:T(8,128)(2,1)}, bf16[256,128]{1,0:T(8,128)(2,1)}, bf16[256,128]{1,0:T(8,128)(2,1)}, f32[640]{0:T(1024)}, f32[128]{0:T(128)}) custom-call(bf16[256,640]{1,0:T(8,128)(2,1)} %get-tuple-element.10.refs_0_, bf16[256,128]{1,0:T(8,128)(2,1)} %get-tuple-element.11.refs_1_, bf16[256,128]{1,0:T(8,128)(2,1)} %get-tuple-element.12.refs_2_, ...), custom_call_target="tpu_custom_call" | custom-call | tf_op jit(solution)/shard_map/pallas_call | solution.py:721

commit v5 on v4

--- a/solution.py
+++ b/solution.py
@@ -454,12 +454,12 @@
     PLACE = {1: 1, 3: 2, 2: 3}
 
     def ring_copy(half, first, place):
-        step = {1: 1, 2: 3, 3: 1 if first else 2}[place]
+        step = {1: 1, 2: 3, 3: 2 if first == 2 else 1}[place]
         return pltpu.make_async_remote_copy(
             src_ref=stage.at[half, first, place],
             dst_ref=gotr.at[half, first, place],
             send_sem=sent.at[1],
-            recv_sem=(far_sem if first and place == 3 else rs_sem).at[half, first],
+            recv_sem=(far_sem if first != 2 and place == 3 else rs_sem).at[half, first],
             device_id=neighbour(half, 1, step),
             device_id_type=pl.DeviceIdType.MESH,
         )
@@ -476,7 +476,7 @@
 
     def ring_send(half, slot):
         first, second = primary_view(half, slot)
-        if second > 1 or (second == 1 and first == 0):
+        if second > 1 or (second == 1 and first == 2):
             stage[half, first, PLACE[second]] = cb[slot, half].astype(BF16)
             ring_copy(half, first, PLACE[second]).start()
 
@@ -488,7 +488,7 @@
             ring_copy(half, first, 1).start()
 
     def ring_sum(half, first):
-        count = 2 if first else 3
+        count = 3 if first == 2 else 2
         finished(gotr.at[half, first, pl.ds(1, count)], rs_sem.at[half, first])
         total = cb[slot_of(half, first, 0), half]
         for place in range(1, count + 1):
@@ -509,11 +509,10 @@
             totals.append(ring_sum(half, first))
             pstage[half, first] = totals[half].astype(BF16)
             last_copy(half, first).start()
-        for half in (LOW, HIGH):
-            gain_part(half, first, totals[half][1] * SCALE)
+        return totals
 
     steps = (15, 14, 13, 12, 11, 7, 9, 8, 6, 5, 10, 4, 3, 2, 1)
-    near = {10: 2, 4: 1, 2: 3}
+    near = {4: 1, 2: 3}
     for slot in steps:
         second_pass(slot)
         for half in (LOW, HIGH):
@@ -521,6 +520,7 @@
         if slot in near:
             near_send(near[slot])
     own_second()
+    partial = {2: last_send(2)}
 
     stat[1, 0] = jnp.zeros((8, SPAN), F32)
     gain_buf[0] = jnp.zeros((8, DH), F32)
@@ -537,21 +537,12 @@
         stat[1, 0, half:half + 1, :] = token_sums(inner)
     stat_send(1)
 
-    for first in (2, 1, 3):
-        last_send(first)
-
-    q_inner = stat_total(1) / D
-    for half in (LOW, HIGH):
-        inner = spread(q_inner[half:half + 1, :])
-        for h in range(GROUP):
-            q_hat = q_ref[offs[half], :, head(h)].astype(F32) * qi[half]
-            sg[half, :, head(h)] = qi[half] * (sg[half, :, head(h)] - q_hat * inner)
+    near_send(0)
+    for first in (1, 3):
+        partial[first] = last_send(first)
 
     first_half = jnp.where(s0 < s1, LOW, HIGH)
     places = ((0, first_half), (1, 1 - first_half))
-    for place, half in places:
-        dq_out[place * SPAN:(place + 1) * SPAN, :] = sg[half].astype(BF16)
-
     def store(number, source, target):
         return pltpu.make_async_copy(source, target, out_sem.at[number])
 
@@ -564,9 +555,10 @@
             )
         )
     ]
-    stores[0].start()
-
     totals = [ring_sum(half, 0) for half in (LOW, HIGH)]
+    for first, pair in partial.items():
+        for half in (LOW, HIGH):
+            gain_part(half, first, pair[half][1] * SCALE)
     for half in (LOW, HIGH):
         gain_part(half, 0, totals[half][1] * SCALE)
 
@@ -600,6 +592,17 @@
     for place, half in places:
         dv_out[place * SPAN:(place + 1) * SPAN, :] = dkn[1, half].astype(BF16)
     stores[2].start()
+
+    q_inner = stat_total(1) / D
+    for half in (LOW, HIGH):
+        inner = spread(q_inner[half:half + 1, :])
+        for h in range(GROUP):
+            q_hat = q_ref[offs[half], :, head(h)].astype(F32) * qi[half]
+            sg[half, :, head(h)] = qi[half] * (sg[half, :, head(h)] - q_hat * inner)
+
+    for place, half in places:
+        dq_out[place * SPAN:(place + 1) * SPAN, :] = sg[half].astype(BF16)
+    stores[0].start()
 
     k_inner = stat_total(2) / KVD
     for half in (LOW, HIGH):

time: 50.8 us -> 50.6 us (level)
  no operation moved by 1% of the time
where the time goes in v5:
time: 50.6 us; the launch traced here: 50.5 us
  Pallas kernels  49.8 us (98%)
  between operations  0.64 us (1%)
    pallas_call x1, Pallas kernels, per_device(): pl.pallas_call(kernel, out_shape=shapes, in_specs=[hbm] * 9, out_specs=(h...  48 us
    pallas_call x1, Pallas kernels, per_device(): pl.pallas_call(pass_on, out_shape=shapes, in_specs=[vmem] * 5, out_specs=...  1.79 us

profile of v5, /device:TPU:1, one launch (start us, length us, event | category | flops | bytes accessed | tf_op | source)
XLA Modules:
  0.0 50.5 jit_solution(3085364808129731361)
XLA Ops:
  0.6 48.0 %shard_map.128 = (bf16[256,640]{1,0:T(8,128)(2,1)}, bf16[256,128]{1,0:T(8,128)(2,1)}, bf16[256,128]{1,0:T(8,128)(2,1)}, f32[640]{0:T(1024)}, f32[128]{0:T(128)}) custom-call(s32[32]{0:T(128)} %so_in.1, bf16[2,128,640]{2,1,0:T(8,128)(2,1)} %bitcast.4, bf16[2,128,128]{2,1,0:T(8,128)(2,1)} %bitcast.6, bf16[2,128,128]{2,1,0:T(8,128)(2,1)} %bitcast.7, ...), custom_call_target="tpu_custom_call" | custom-call | tf_op jit(solution)/shard_map/pallas_call | solution.py:709
  48.7 1.8 %shard_map.129 = (bf16[256,640]{1,0:T(8,128)(2,1)}, bf16[256,128]{1,0:T(8,128)(2,1)}, bf16[256,128]{1,0:T(8,128)(2,1)}, f32[640]{0:T(1024)}, f32[128]{0:T(128)}) custom-call(bf16[256,640]{1,0:T(8,128)(2,1)} %get-tuple-element.10.refs_0_, bf16[256,128]{1,0:T(8,128)(2,1)} %get-tuple-element.11.refs_1_, bf16[256,128]{1,0:T(8,128)(2,1)} %get-tuple-element.12.refs_2_, ...), custom_call_target="tpu_custom_call" | custom-call | tf_op jit(solution)/shard_map/pallas_call | solution.py:724

commit v6 on v5

--- a/solution.py
+++ b/solution.py
@@ -604,15 +604,6 @@
         dq_out[place * SPAN:(place + 1) * SPAN, :] = sg[half].astype(BF16)
     stores[0].start()
 
-    k_inner = stat_total(2) / KVD
-    for half in (LOW, HIGH):
-        inner = spread(k_inner[half:half + 1, :])
-        k_hat = kv[half, 0, KEY].astype(F32) * ki[half]
-        dkn[0, half] = ki[half] * (dkn[0, half] - k_hat * inner)
-    for place, half in places:
-        dk_out[place * SPAN:(place + 1) * SPAN, :] = dkn[0, half].astype(BF16)
-    stores[1].start()
-
     finished(gain_buf.at[pl.ds(1, SLOTS - 1)], small_sem.at[1])
     total = gain_buf[0]
     for slot in range(1, SLOTS):
@@ -622,13 +613,22 @@
     dkg_out[...] = total[5:6, :].reshape(DH)
     stores[3].start()
     stores[4].start()
-
     finished(kv.at[:, pl.ds(0, SLOTS - 1)], sent.at[0])
     finished(stage.at[:, :, pl.ds(1, 3)], sent.at[1])
     finished(pstage.at[:, pl.ds(1, 3)], sent.at[2])
-    finished(stat.at[:, pl.ds(1, 7)], sent.at[3])
     finished(inv_buf.at[pl.ds(1, SLOTS - 1)], sent.at[4])
     finished(gain_buf.at[pl.ds(1, SLOTS - 1)], sent.at[5])
+
+    k_inner = stat_total(2) / KVD
+    for half in (LOW, HIGH):
+        inner = spread(k_inner[half:half + 1, :])
+        k_hat = kv[half, 0, KEY].astype(F32) * ki[half]
+        dkn[0, half] = ki[half] * (dkn[0, half] - k_hat * inner)
+    for place, half in places:
+        dk_out[place * SPAN:(place + 1) * SPAN, :] = dkn[0, half].astype(BF16)
+    stores[1].start()
+
+    finished(stat.at[:, pl.ds(1, 7)], sent.at[3])
     for item in stores:
         item.wait()
 

time: 50.6 us -> 50.6 us (level)
  no operation moved by 1% of the time
where the time goes in v6:
time: 50.6 us; the launch traced here: 50.4 us
  Pallas kernels  49.8 us (98%)
  between operations  0.64 us (1%)
    pallas_call x1, Pallas kernels, per_device(): pl.pallas_call(kernel, out_shape=shapes, in_specs=[hbm] * 9, out_specs=(h...  48 us
    pallas_call x1, Pallas kernels, per_device(): pl.pallas_call(pass_on, out_shape=shapes, in_specs=[vmem] * 5, out_specs=...  1.79 us

profile of v6, /device:TPU:1, one launch (start us, length us, event | category | flops | bytes accessed | tf_op | source)
XLA Modules:
  0.0 50.4 jit_solution(7949454893179325896)
XLA Ops:
  0.6 48.0 %shard_map.128 = (bf16[256,640]{1,0:T(8,128)(2,1)}, bf16[256,128]{1,0:T(8,128)(2,1)}, bf16[256,128]{1,0:T(8,128)(2,1)}, f32[640]{0:T(1024)}, f32[128]{0:T(128)}) custom-call(s32[32]{0:T(128)} %so_in.1, bf16[2,128,640]{2,1,0:T(8,128)(2,1)} %bitcast.4, bf16[2,128,128]{2,1,0:T(8,128)(2,1)} %bitcast.6, bf16[2,128,128]{2,1,0:T(8,128)(2,1)} %bitcast.7, ...), custom_call_target="tpu_custom_call" | custom-call | tf_op jit(solution)/shard_map/pallas_call | solution.py:709
  48.6 1.8 %shard_map.129 = (bf16[256,640]{1,0:T(8,128)(2,1)}, bf16[256,128]{1,0:T(8,128)(2,1)}, bf16[256,128]{1,0:T(8,128)(2,1)}, f32[640]{0:T(1024)}, f32[128]{0:T(128)}) custom-call(bf16[256,640]{1,0:T(8,128)(2,1)} %get-tuple-element.10.refs_0_, bf16[256,128]{1,0:T(8,128)(2,1)} %get-tuple-element.11.refs_1_, bf16[256,128]{1,0:T(8,128)(2,1)} %get-tuple-element.12.refs_2_, ...), custom_call_target="tpu_custom_call" | custom-call | tf_op jit(solution)/shard_map/pallas_call | solution.py:724
